TPU v7x, 512 devices: a whole 4x8x8 slice. The times are simulated.
512 devices in a mesh: slab: 64 (over z, y_lo, core), sub: 8 (over x, y_hi).
Axes of the slice: x: 4, y: 8 (y_hi: 2, y_lo: 4; y = y_hi * 4 + y_lo), z: 8, core: 2. Of those that a mesh axis runs over, the one named last changes fastest.
Arguments:
- fields: float32 [3, 3, 3, 3, 128, 64, 128], P(None, None, None, None, 'slab', 'sub'), may hold values from 0.25 to 4
- speeds: float32 [3, 128, 64, 128], P(None, 'slab', 'sub'), may hold values from -4.5 to 4.5
Outputs:
- remapped: float32 [3, 3, 3, 3, 128, 64, 128], P(None, None, None, None, 'slab', 'sub')
All inputs are finite; a program needn't handle non-finite values. Where the computation divides by a largest or mean magnitude, that divisor is 1e-20 or more.
Results may differ from a plain program's by a relative error of at most 0.0001.
Values sent between devices are 32-bit elements; how exact they have to be, the bound alone decides.
A program may use at most 64 MiB of HBM per device.

v0:
```python
import jax
import jax.numpy as jnp
from jax import lax
from jax.sharding import PartitionSpec as P

STEPS = 3


DERIVATIVE = ((-1.5, 2.0, -0.5), (-0.5, 0.0, 0.5), (0.5, -2.0, 1.5))
QUAD_WEIGHTS = (1.0 / 3.0, 4.0 / 3.0, 1.0 / 3.0)
COURANT = 0.12
SOFTNESS = 0.05


def extended(block, sides, width):
    for axis, dim in sides:
        count = lax.axis_size(axis)
        forward = [(i, i + 1) for i in range(count - 1)]
        forward.append((count - 1, 0))
        backward = [(target, source) for source, target in forward]
        low = lax.ppermute(
            lax.slice_in_dim(block, block.shape[dim] - width, None, axis=dim), axis, forward
        )
        high = lax.ppermute(lax.slice_in_dim(block, 0, width, axis=dim), axis, backward)
        block = jnp.concatenate([low, block, high], axis=dim)
    return block


def from_behind(array, axis, by):
    length = lax.axis_size(axis)
    return lax.ppermute(array, axis, [(i, (i + by) % length) for i in range(length)])


def direction_term(values, interior, speed_lo, speed_hi, neighbour_low, neighbour_high, node_axis):
    node_slices = [lax.slice_in_dim(values, i, i + 1, axis=node_axis) for i in range(3)]
    face_low = node_slices[0]
    face_high = node_slices[2]
    flux_lo = jnp.maximum(speed_lo, 0.0) * neighbour_low + jnp.minimum(speed_lo, 0.0) * face_low
    flux_hi = jnp.maximum(speed_hi, 0.0) * face_high + jnp.minimum(speed_hi, 0.0) * neighbour_high
    outputs = []
    for i in range(3):
        gradient = (
            DERIVATIVE[i][0] * node_slices[0]
            + DERIVATIVE[i][1] * node_slices[1]
            + DERIVATIVE[i][2] * node_slices[2]
        )
        contrib = interior * gradient
        if i == 2:
            contrib = contrib + 3.0 * (flux_hi - interior * face_high)
        if i == 0:
            contrib = contrib - 3.0 * (flux_lo - interior * face_low)
        outputs.append(-2.0 * contrib)
    return jnp.concatenate(outputs, axis=node_axis)


def gather_rims(values):
    ghosted = extended(values, (("slab", 4), ("sub", 5)), 1)
    neighbour_rims = (
        ghosted[:, 2:3, :, :, 0:1, 1:-1, :],
        ghosted[:, 0:1, :, :, -1:, 1:-1, :],
        ghosted[:, :, 2:3, :, 1:-1, 0:1, :],
        ghosted[:, :, 0:1, :, 1:-1, -1:, :],
    )
    return (neighbour_rims, ghosted)


def tendency(values, neighbour_rims, speed_lows, speed_highs, interiors):
    high_x = values[:, 2:3]
    low_x = values[:, 0:1]
    neighbour_low_x = jnp.concatenate([neighbour_rims[0], high_x[:, :, :, :, :-1]], axis=4)
    neighbour_high_x = jnp.concatenate([low_x[:, :, :, :, 1:], neighbour_rims[1]], axis=4)
    summed = direction_term(
        values, interiors[0], speed_lows[0], speed_highs[0], neighbour_low_x, neighbour_high_x, 1
    )
    high_y = values[:, :, 2:3]
    low_y = values[:, :, 0:1]
    neighbour_low_y = jnp.concatenate([neighbour_rims[2], high_y[:, :, :, :, :, :-1]], axis=5)
    neighbour_high_y = jnp.concatenate([low_y[:, :, :, :, :, 1:], neighbour_rims[3]], axis=5)
    summed = summed + direction_term(
        values, interiors[1], speed_lows[1], speed_highs[1], neighbour_low_y, neighbour_high_y, 2
    )
    high_z = values[:, :, :, 2:3]
    low_z = values[:, :, :, 0:1]
    neighbour_low_z = jnp.roll(high_z, 1, axis=6)
    neighbour_high_z = jnp.roll(low_z, -1, axis=6)
    summed = summed + direction_term(
        values, interiors[2], speed_lows[2], speed_highs[2], neighbour_low_z, neighbour_high_z, 3
    )
    return summed


def bounds_from_extended(extended_low, extended_high):
    center_low = extended_low[:, 1:-1, 1:-1, :]
    center_high = extended_high[:, 1:-1, 1:-1, :]
    lowest = center_low
    highest = center_high
    for source_low, source_high in (
        (extended_low[:, :-2, 1:-1, :], extended_high[:, :-2, 1:-1, :]),
        (extended_low[:, 2:, 1:-1, :], extended_high[:, 2:, 1:-1, :]),
        (extended_low[:, 1:-1, :-2, :], extended_high[:, 1:-1, :-2, :]),
        (extended_low[:, 1:-1, 2:, :], extended_high[:, 1:-1, 2:, :]),
        (jnp.roll(center_low, 1, axis=3), jnp.roll(center_high, 1, axis=3)),
        (jnp.roll(center_low, -1, axis=3), jnp.roll(center_high, -1, axis=3)),
    ):
        lowest = jnp.minimum(lowest, source_low)
        highest = jnp.maximum(highest, source_high)
    return (lowest, highest)


def limiter(values, lowest, highest):
    weight_line = jnp.array(QUAD_WEIGHTS, dtype=values.dtype)
    weights = (
        weight_line[:, None, None] * weight_line[None, :, None] * weight_line[None, None, :] / 8.0
    )[None, :, :, :, None, None, None]
    average = jnp.sum(values * weights, axis=(1, 2, 3), keepdims=True)
    largest = jnp.max(values, axis=(1, 2, 3), keepdims=True)
    smallest = jnp.min(values, axis=(1, 2, 3), keepdims=True)
    upper_ratio = (jnp.maximum(highest[:, None, None, None] - average, 0.0) + SOFTNESS) / (
        largest - average + SOFTNESS
    )
    lower_ratio = (jnp.maximum(average - lowest[:, None, None, None], 0.0) + SOFTNESS) / (
        average - smallest + SOFTNESS
    )
    scaling = jnp.minimum(1.0, jnp.minimum(upper_ratio, lower_ratio))
    return average + scaling * (values - average)


def on_device(fields, speeds):
    upper_row = from_behind(speeds[0, 0:1], "slab", -1)
    upper_column = from_behind(speeds[1, :, 0:1], "sub", -1)
    speed_lows = [speeds[0], speeds[1], speeds[2]]
    speed_highs = [
        jnp.concatenate([speeds[0, 1:], upper_row], axis=0),
        jnp.concatenate([speeds[1, :, 1:], upper_column], axis=1),
        jnp.roll(speeds[2], -1, axis=2),
    ]
    interiors = [0.5 * (speed_lows[d] + speed_highs[d]) for d in range(3)]
    local_fast = jnp.max(jnp.abs(interiors[0]) + jnp.abs(interiors[1]) + jnp.abs(interiors[2]))
    fastest = lax.pmax(local_fast, ("slab", "sub"))
    time_step = COURANT / (fastest + 1e-06)
    current = fields
    for count in range(STEPS):
        neighbour_rims, ghosted = gather_rims(current)
        lowest, highest = bounds_from_extended(
            jnp.min(ghosted, axis=(1, 2, 3)), jnp.max(ghosted, axis=(1, 2, 3))
        )
        section_one = limiter(
            current
            + time_step * tendency(current, neighbour_rims, speed_lows, speed_highs, interiors),
            lowest,
            highest,
        )
        rims_one, unused_one = gather_rims(section_one)
        section_two = limiter(
            0.75 * current
            + 0.25
            * (
                section_one
                + time_step * tendency(section_one, rims_one, speed_lows, speed_highs, interiors)
            ),
            lowest,
            highest,
        )
        rims_two, unused_two = gather_rims(section_two)
        current = limiter(
            current / 3.0
            + 2.0
            / 3.0
            * (
                section_two
                + time_step * tendency(section_two, rims_two, speed_lows, speed_highs, interiors)
            ),
            lowest,
            highest,
        )
    return current


def solution(mesh):
    return jax.shard_map(
        on_device,
        mesh=mesh,
        in_specs=(P(None, None, None, None, "slab", "sub", None), P(None, "slab", "sub", None)),
        out_specs=P(None, None, None, None, "slab", "sub", None),
        check_vma=False,
    )
```

profile of v0, /device:TPU:1, one launch (start us, length us, event | category | flops | bytes accessed | tf_op | source)
XLA Modules:
  0.0 452.6 jit_solution(17891531750209560099)
XLA Ops:
  0.7 10.5 %collective-permute-start.1 = (f32[2,1,128]{2,1,0:T(1,128)S(1)}, f32[2,1,128]{2,1,0:T(1,128)S(1)}, u32[]{:S(2)}, u32[]{:S(2)}) collective-permute-start(f32[2,1,128]{2,1,0:T(1,128)S(1)} %slice_bitcast_fusion.4), channel_id=1, source_target_pairs={{0,7},{1,0},{2,1},{3,2},{4,3},{5,4},{6,5},{7,6},{8,15},{9,8},{10,9... | collective-permute-start | bytes 3080 | tf_op jit(solution)/shard_map/ppermute | solution.py:31
  19.5 9.7 %collective-permute-start.3 = (f32[3,3,3,3,1,8,128]{6,5,4,3,2,1,0:T(8,128)}, f32[3,3,3,3,1,8,128]{6,5,4,3,2,1,0:T(8,128)S(1)}, u32[]{:S(2)}, u32[]{:S(2)}) collective-permute-start(f32[3,3,3,3,1,8,128]{6,5,4,3,2,1,0:T(8,128)} %get-tuple-element.244), channel_id=1, source_target_pairs={{8,0},{16,8},{24,16},{32,24},{40,32},{48,40},{56,48},{64,56},{72,6... | collective-permute-start | bytes 995336 | tf_op jit(solution)/shard_map/ppermute | solution.py:24
  32.1 97.2 %pmax.7 = f32[]{:T(128)} all-reduce(f32[]{:T(128)} %get-tuple-element.288), channel_id=1, replica_groups=mesh['slab'=64,'sub'=8] {'slab','sub'}, use_global_device_ids=true, to_apply=%region_1.2 | all-reduce | flops 1 | bytes 8 | tf_op jit(solution)/shard_map/pmax | solution.py:139
  130.5 5.6 %collective-permute-start.4 = (f32[3,3,3,3,4,1,128]{6,4,5,3,2,1,0:T(4,128)S(1)}, f32[3,3,3,3,4,1,128]{6,4,5,3,2,1,0:T(4,128)S(1)}, u32[]{:S(2)}, u32[]{:S(2)}) collective-permute-start(f32[3,3,3,3,4,1,128]{6,4,5,3,2,1,0:T(4,128)S(1)} %get-tuple-element.76), channel_id=1, source_target_pairs={{0,1},{1,2},{2,3},{3,4},{4,5},{5,6},{6,7},{7,0},{8,9},{9,10},{10,1... | collective-permute-start | bytes 497672 | tf_op jit(solution)/shard_map/ppermute | solution.py:21
  136.1 5.7 %collective-permute-start.5 = (f32[3,3,3,3,4,1,128]{6,4,5,3,2,1,0:T(4,128)S(1)}, f32[3,3,3,3,4,1,128]{6,4,5,3,2,1,0:T(4,128)S(1)}, u32[]{:S(2)}, u32[]{:S(2)}) collective-permute-start(f32[3,3,3,3,4,1,128]{6,4,5,3,2,1,0:T(4,128)S(1)} %get-tuple-element.77), channel_id=1, source_target_pairs={{1,0},{2,1},{3,2},{4,3},{5,4},{6,5},{7,6},{0,7},{9,8},{10,9},{11,1... | collective-permute-start | bytes 497672 | tf_op jit(solution)/shard_map/ppermute | solution.py:24
  142.1 7.4 %collective-permute-done.4 = f32[3,3,3,3,4,1,128]{6,4,5,3,2,1,0:T(4,128)S(1)} collective-permute-done((f32[3,3,3,3,4,1,128]{6,4,5,3,2,1,0:T(4,128)S(1)}, f32[3,3,3,3,4,1,128]{6,4,5,3,2,1,0:T(4,128)S(1)}, u32[]{:S(2)}, u32[]{:S(2)}) %collective-permute-start.4) | collective-permute-done | bytes 165920 | tf_op jit(solution)/shard_map/ppermute | solution.py:21
  154.7 6.3 %collective-permute-start.6 = (f32[3,3,3,3,1,8,128]{6,5,4,3,2,1,0:T(8,128)S(1)}, f32[3,3,3,3,1,8,128]{6,5,4,3,2,1,0:T(8,128)S(1)}, u32[]{:S(2)}, u32[]{:S(2)}) collective-permute-start(f32[3,3,3,3,1,8,128]{6,5,4,3,2,1,0:T(8,128)S(1)} %get-tuple-element.233), channel_id=1, source_target_pairs={{0,8},{8,16},{16,24},{24,32},{32,40},{40,48},{48,56},{56,64},{64,7... | collective-permute-start | bytes 995336 | tf_op jit(solution)/shard_map/ppermute | solution.py:21
  165.1 6.9 %collective-permute-done.7 = f32[3,3,3,3,1,8,128]{6,5,4,3,2,1,0:T(8,128)S(1)} collective-permute-done((f32[3,3,3,3,1,8,128]{6,5,4,3,2,1,0:T(8,128)S(1)}, f32[3,3,3,3,1,8,128]{6,5,4,3,2,1,0:T(8,128)S(1)}, u32[]{:S(2)}, u32[]{:S(2)}) %collective-permute-start.7) | collective-permute-done | bytes 331808 | tf_op jit(solution)/shard_map/ppermute | solution.py:24
  172.2 5.5 %collective-permute-start.9 = (f32[3,3,3,3,4,1,128]{6,4,5,3,2,1,0:T(4,128)S(1)}, f32[3,3,3,3,4,1,128]{6,4,5,3,2,1,0:T(4,128)S(1)}, u32[]{:S(2)}, u32[]{:S(2)}) collective-permute-start(f32[3,3,3,3,4,1,128]{6,4,5,3,2,1,0:T(4,128)S(1)} %bitcast.91), channel_id=1, source_target_pairs={{1,0},{2,1},{3,2},{4,3},{5,4},{6,5},{7,6},{0,7},{9,8},{10,9},{11,1... | collective-permute-start | bytes 497672 | tf_op jit(solution)/shard_map/ppermute | solution.py:24
  183.4 9.6 %collective-permute-done.8 = f32[3,3,3,3,4,1,128]{6,4,5,3,2,1,0:T(4,128)S(1)} collective-permute-done((f32[3,3,3,3,4,1,128]{6,4,5,3,2,1,0:T(4,128)S(1)}, f32[3,3,3,3,4,1,128]{6,4,5,3,2,1,0:T(4,128)S(1)}, u32[]{:S(2)}, u32[]{:S(2)}) %collective-permute-start.8) | collective-permute-done | bytes 165920 | tf_op jit(solution)/shard_map/ppermute | solution.py:21
  194.2 6.6 %collective-permute-start.10 = (f32[3,3,3,3,1,8,128]{6,5,4,3,2,1,0:T(8,128)S(1)}, f32[3,3,3,3,1,8,128]{6,5,4,3,2,1,0:T(8,128)S(1)}, u32[]{:S(2)}, u32[]{:S(2)}) collective-permute-start(f32[3,3,3,3,1,8,128]{6,5,4,3,2,1,0:T(8,128)S(1)} %get-tuple-element.223), channel_id=1, source_target_pairs={{0,8},{8,16},{16,24},{24,32},{32,40},{40,48},{48,56},{56,64},{64,7... | collective-permute-start | bytes 995336 | tf_op jit(solution)/shard_map/ppermute | solution.py:21
  213.1 5.6 %collective-permute-start.12 = (f32[3,3,3,3,4,1,128]{6,4,5,3,2,1,0:T(4,128)S(1)}, f32[3,3,3,3,4,1,128]{6,4,5,3,2,1,0:T(4,128)S(1)}, u32[]{:S(2)}, u32[]{:S(2)}) collective-permute-start(f32[3,3,3,3,4,1,128]{6,4,5,3,2,1,0:T(4,128)S(1)} %bitcast.84), channel_id=1, source_target_pairs={{0,1},{1,2},{2,3},{3,4},{4,5},{5,6},{6,7},{7,0},{8,9},{9,10},{10,1... | collective-permute-start | bytes 497672 | tf_op jit(solution)/shard_map/ppermute | solution.py:21
  221.7 6.2 %collective-permute-done.12 = f32[3,3,3,3,4,1,128]{6,4,5,3,2,1,0:T(4,128)S(1)} collective-permute-done((f32[3,3,3,3,4,1,128]{6,4,5,3,2,1,0:T(4,128)S(1)}, f32[3,3,3,3,4,1,128]{6,4,5,3,2,1,0:T(4,128)S(1)}, u32[]{:S(2)}, u32[]{:S(2)}) %collective-permute-start.12) | collective-permute-done | bytes 165920 | tf_op jit(solution)/shard_map/ppermute | solution.py:21
  229.1 5.6 %collective-permute-start.14 = (f32[3,3,3,3,1,8,128]{6,5,4,3,2,1,0:T(8,128)S(1)}, f32[3,3,3,3,1,8,128]{6,5,4,3,2,1,0:T(8,128)S(1)}, u32[]{:S(2)}, u32[]{:S(2)}) collective-permute-start(f32[3,3,3,3,1,8,128]{6,5,4,3,2,1,0:T(8,128)S(1)} %get-tuple-element.213), channel_id=1, source_target_pairs={{0,8},{8,16},{16,24},{24,32},{32,40},{40,48},{48,56},{56,64},{64,7... | collective-permute-start | bytes 995336 | tf_op jit(solution)/shard_map/ppermute | solution.py:21
  238.7 7.1 %collective-permute-done.15 = f32[3,3,3,3,1,8,128]{6,5,4,3,2,1,0:T(8,128)S(1)} collective-permute-done((f32[3,3,3,3,1,8,128]{6,5,4,3,2,1,0:T(8,128)S(1)}, f32[3,3,3,3,1,8,128]{6,5,4,3,2,1,0:T(8,128)S(1)}, u32[]{:S(2)}, u32[]{:S(2)}) %collective-permute-start.15) | collective-permute-done | bytes 331808 | tf_op jit(solution)/shard_map/ppermute | solution.py:24
  248.0 7.5 %collective-permute-start.16 = (f32[3,3,3,3,4,1,128]{6,4,5,3,2,1,0:T(4,128)S(1)}, f32[3,3,3,3,4,1,128]{6,4,5,3,2,1,0:T(4,128)S(1)}, u32[]{:S(2)}, u32[]{:S(2)}) collective-permute-start(f32[3,3,3,3,4,1,128]{6,4,5,3,2,1,0:T(4,128)S(1)} %bitcast.89), channel_id=1, source_target_pairs={{0,1},{1,2},{2,3},{3,4},{4,5},{5,6},{6,7},{7,0},{8,9},{9,10},{10,1... | collective-permute-start | bytes 497672 | tf_op jit(solution)/shard_map/ppermute | solution.py:21
  272.0 8.0 %collective-permute-done.19 = f32[3,3,3,3,1,8,128]{6,5,4,3,2,1,0:T(8,128)S(1)} collective-permute-done((f32[3,3,3,3,1,8,128]{6,5,4,3,2,1,0:T(8,128)S(1)}, f32[3,3,3,3,1,8,128]{6,5,4,3,2,1,0:T(8,128)S(1)}, u32[]{:S(2)}, u32[]{:S(2)}) %collective-permute-start.19) | collective-permute-done | bytes 331808 | tf_op jit(solution)/shard_map/ppermute | solution.py:24
  280.2 5.5 %collective-permute-start.21 = (f32[3,3,3,3,4,1,128]{6,4,5,3,2,1,0:T(4,128)S(1)}, f32[3,3,3,3,4,1,128]{6,4,5,3,2,1,0:T(4,128)S(1)}, u32[]{:S(2)}, u32[]{:S(2)}) collective-permute-start(f32[3,3,3,3,4,1,128]{6,4,5,3,2,1,0:T(4,128)S(1)} %bitcast.93), channel_id=1, source_target_pairs={{1,0},{2,1},{3,2},{4,3},{5,4},{6,5},{7,6},{0,7},{9,8},{10,9},{11,1... | collective-permute-start | bytes 497672 | tf_op jit(solution)/shard_map/ppermute | solution.py:24
  294.1 11.0 %collective-permute-done.20 = f32[3,3,3,3,4,1,128]{6,4,5,3,2,1,0:T(4,128)S(1)} collective-permute-done((f32[3,3,3,3,4,1,128]{6,4,5,3,2,1,0:T(4,128)S(1)}, f32[3,3,3,3,4,1,128]{6,4,5,3,2,1,0:T(4,128)S(1)}, u32[]{:S(2)}, u32[]{:S(2)}) %collective-permute-start.20) | collective-permute-done | bytes 165920 | tf_op jit(solution)/shard_map/ppermute | solution.py:21
  312.3 8.2 %collective-permute-done.23 = f32[3,3,3,3,1,8,128]{6,5,4,3,2,1,0:T(8,128)S(1)} collective-permute-done((f32[3,3,3,3,1,8,128]{6,5,4,3,2,1,0:T(8,128)S(1)}, f32[3,3,3,3,1,8,128]{6,5,4,3,2,1,0:T(8,128)S(1)}, u32[]{:S(2)}, u32[]{:S(2)}) %collective-permute-start.23) | collective-permute-done | bytes 331808 | tf_op jit(solution)/shard_map/ppermute | solution.py:24
  330.2 9.0 %collective-permute-done.25 = f32[3,3,3,3,4,1,128]{6,4,5,3,2,1,0:T(4,128)S(1)} collective-permute-done((f32[3,3,3,3,4,1,128]{6,4,5,3,2,1,0:T(4,128)S(1)}, f32[3,3,3,3,4,1,128]{6,4,5,3,2,1,0:T(4,128)S(1)}, u32[]{:S(2)}, u32[]{:S(2)}) %collective-permute-start.25) | collective-permute-done | bytes 165920 | tf_op jit(solution)/shard_map/ppermute | solution.py:24
  340.8 7.1 %collective-permute-start.26 = (f32[3,3,3,3,1,8,128]{6,5,4,3,2,1,0:T(8,128)S(1)}, f32[3,3,3,3,1,8,128]{6,5,4,3,2,1,0:T(8,128)S(1)}, u32[]{:S(2)}, u32[]{:S(2)}) collective-permute-start(f32[3,3,3,3,1,8,128]{6,5,4,3,2,1,0:T(8,128)S(1)} %get-tuple-element.183), channel_id=1, source_target_pairs={{0,8},{8,16},{16,24},{24,32},{32,40},{40,48},{48,56},{56,64},{64,7... | collective-permute-start | bytes 995336 | tf_op jit(solution)/shard_map/ppermute | solution.py:21
  360.0 6.3 %collective-permute-start.28 = (f32[3,3,3,3,4,1,128]{6,4,5,3,2,1,0:T(4,128)S(1)}, f32[3,3,3,3,4,1,128]{6,4,5,3,2,1,0:T(4,128)S(1)}, u32[]{:S(2)}, u32[]{:S(2)}) collective-permute-start(f32[3,3,3,3,4,1,128]{6,4,5,3,2,1,0:T(4,128)S(1)} %bitcast.90), channel_id=1, source_target_pairs={{0,1},{1,2},{2,3},{3,4},{4,5},{5,6},{6,7},{7,0},{8,9},{9,10},{10,1... | collective-permute-start | bytes 497672 | tf_op jit(solution)/shard_map/ppermute | solution.py:21
  366.6 5.8 %collective-permute-done.29 = f32[3,3,3,3,4,1,128]{6,4,5,3,2,1,0:T(4,128)S(1)} collective-permute-done((f32[3,3,3,3,4,1,128]{6,4,5,3,2,1,0:T(4,128)S(1)}, f32[3,3,3,3,4,1,128]{6,4,5,3,2,1,0:T(4,128)S(1)}, u32[]{:S(2)}, u32[]{:S(2)}) %collective-permute-start.29) | collective-permute-done | bytes 165920 | tf_op jit(solution)/shard_map/ppermute | solution.py:24
  376.3 5.3 %collective-permute-start.30 = (f32[3,3,3,3,1,8,128]{6,5,4,3,2,1,0:T(8,128)S(1)}, f32[3,3,3,3,1,8,128]{6,5,4,3,2,1,0:T(8,128)S(1)}, u32[]{:S(2)}, u32[]{:S(2)}) collective-permute-start(f32[3,3,3,3,1,8,128]{6,5,4,3,2,1,0:T(8,128)S(1)} %get-tuple-element.173), channel_id=1, source_target_pairs={{0,8},{8,16},{16,24},{24,32},{32,40},{40,48},{48,56},{56,64},{64,7... | collective-permute-start | bytes 995336 | tf_op jit(solution)/shard_map/ppermute | solution.py:21
  385.7 8.0 %collective-permute-done.31 = f32[3,3,3,3,1,8,128]{6,5,4,3,2,1,0:T(8,128)S(1)} collective-permute-done((f32[3,3,3,3,1,8,128]{6,5,4,3,2,1,0:T(8,128)S(1)}, f32[3,3,3,3,1,8,128]{6,5,4,3,2,1,0:T(8,128)S(1)}, u32[]{:S(2)}, u32[]{:S(2)}) %collective-permute-start.31) | collective-permute-done | bytes 331808 | tf_op jit(solution)/shard_map/ppermute | solution.py:24
  393.9 6.8 %collective-permute-start.33 = (f32[3,3,3,3,4,1,128]{6,4,5,3,2,1,0:T(4,128)S(1)}, f32[3,3,3,3,4,1,128]{6,4,5,3,2,1,0:T(4,128)S(1)}, u32[]{:S(2)}, u32[]{:S(2)}) collective-permute-start(f32[3,3,3,3,4,1,128]{6,4,5,3,2,1,0:T(4,128)S(1)} %bitcast.95), channel_id=1, source_target_pairs={{1,0},{2,1},{3,2},{4,3},{5,4},{6,5},{7,6},{0,7},{9,8},{10,9},{11,1... | collective-permute-start | bytes 497672 | tf_op jit(solution)/shard_map/ppermute | solution.py:24
  406.1 6.7 %collective-permute-done.32 = f32[3,3,3,3,4,1,128]{6,4,5,3,2,1,0:T(4,128)S(1)} collective-permute-done((f32[3,3,3,3,4,1,128]{6,4,5,3,2,1,0:T(4,128)S(1)}, f32[3,3,3,3,4,1,128]{6,4,5,3,2,1,0:T(4,128)S(1)}, u32[]{:S(2)}, u32[]{:S(2)}) %collective-permute-start.32) | collective-permute-done | bytes 165920 | tf_op jit(solution)/shard_map/ppermute | solution.py:21
  414.1 5.5 %collective-permute-start.34 = (f32[3,3,3,3,1,8,128]{6,5,4,3,2,1,0:T(8,128)S(1)}, f32[3,3,3,3,1,8,128]{6,5,4,3,2,1,0:T(8,128)S(1)}, u32[]{:S(2)}, u32[]{:S(2)}) collective-permute-start(f32[3,3,3,3,1,8,128]{6,5,4,3,2,1,0:T(8,128)S(1)} %get-tuple-element.163), channel_id=1, source_target_pairs={{0,8},{8,16},{16,24},{24,32},{32,40},{40,48},{48,56},{56,64},{64,7... | collective-permute-start | bytes 995336 | tf_op jit(solution)/shard_map/ppermute | solution.py:21
  423.6 5.8 %collective-permute-done.35 = f32[3,3,3,3,1,8,128]{6,5,4,3,2,1,0:T(8,128)S(1)} collective-permute-done((f32[3,3,3,3,1,8,128]{6,5,4,3,2,1,0:T(8,128)S(1)}, f32[3,3,3,3,1,8,128]{6,5,4,3,2,1,0:T(8,128)S(1)}, u32[]{:S(2)}, u32[]{:S(2)}) %collective-permute-start.35) | collective-permute-done | bytes 331808 | tf_op jit(solution)/shard_map/ppermute | solution.py:24
  433.0 5.9 %collective-permute-start.36 = (f32[3,3,3,3,4,1,128]{6,4,5,3,2,1,0:T(4,128)S(1)}, f32[3,3,3,3,4,1,128]{6,4,5,3,2,1,0:T(4,128)S(1)}, u32[]{:S(2)}, u32[]{:S(2)}) collective-permute-start(f32[3,3,3,3,4,1,128]{6,4,5,3,2,1,0:T(4,128)S(1)} %bitcast.82), channel_id=1, source_target_pairs={{0,1},{1,2},{2,3},{3,4},{4,5},{5,6},{6,7},{7,0},{8,9},{9,10},{10,1... | collective-permute-start | bytes 497672 | tf_op jit(solution)/shard_map/ppermute | solution.py:21
  442.6 8.2 %collective-permute-done.36 = f32[3,3,3,3,4,1,128]{6,4,5,3,2,1,0:T(4,128)S(1)} collective-permute-done((f32[3,3,3,3,4,1,128]{6,4,5,3,2,1,0:T(4,128)S(1)}, f32[3,3,3,3,4,1,128]{6,4,5,3,2,1,0:T(4,128)S(1)}, u32[]{:S(2)}, u32[]{:S(2)}) %collective-permute-start.36) | collective-permute-done | bytes 165920 | tf_op jit(solution)/shard_map/ppermute | solution.py:21
  (230 shorter events, 134.7 us)
Async XLA Ops:
  0.7 30.6 %collective-permute-start.1 = (f32[2,1,128]{2,1,0:T(1,128)S(1)}, f32[2,1,128]{2,1,0:T(1,128)S(1)}, u32[]{:S(2)}, u32[]{:S(2)}) collective-permute-start(f32[2,1,128]{2,1,0:T(1,128)S(1)} %slice_bitcast_fusion.4), channel_id=1, source_target_pairs={{0,7},{1,0},{2,1},{3,2},{4,3},{5,4},{6,5},{7,6},{8,15},{9,8},{10,9... | collective-permute-start | bytes 3080 | tf_op jit(solution)/shard_map/ppermute | solution.py:31
  11.9 19.4 %collective-permute-start = (f32[1,8,128]{2,1,0:T(8,128)S(1)}, f32[1,8,128]{2,1,0:T(8,128)S(1)}, u32[]{:S(2)}, u32[]{:S(2)}) collective-permute-start(f32[1,8,128]{2,1,0:T(8,128)S(1)} %get-tuple-element.294), channel_id=1, source_target_pairs={{0,504},{8,0},{16,8},{24,16},{32,24},{40,32},{48,40},{56,48},{64,5... | collective-permute-start | bytes 12296 | tf_op jit(solution)/shard_map/ppermute | solution.py:31
  16.8 113.4 %collective-permute-start.2 = (f32[3,3,3,3,1,8,128]{6,5,4,3,2,1,0:T(8,128)}, f32[3,3,3,3,1,8,128]{6,5,4,3,2,1,0:T(8,128)S(1)}, u32[]{:S(2)}, u32[]{:S(2)}) collective-permute-start(f32[3,3,3,3,1,8,128]{6,5,4,3,2,1,0:T(8,128)} %get-tuple-element.243), channel_id=1, source_target_pairs={{0,8},{8,16},{16,24},{24,32},{32,40},{40,48},{48,56},{56,64},{64,7... | collective-permute-start | bytes 995336 | tf_op jit(solution)/shard_map/ppermute | solution.py:21
  19.5 110.7 %collective-permute-start.3 = (f32[3,3,3,3,1,8,128]{6,5,4,3,2,1,0:T(8,128)}, f32[3,3,3,3,1,8,128]{6,5,4,3,2,1,0:T(8,128)S(1)}, u32[]{:S(2)}, u32[]{:S(2)}) collective-permute-start(f32[3,3,3,3,1,8,128]{6,5,4,3,2,1,0:T(8,128)} %get-tuple-element.244), channel_id=1, source_target_pairs={{8,0},{16,8},{24,16},{32,24},{40,32},{48,40},{56,48},{64,56},{72,6... | collective-permute-start | bytes 995336 | tf_op jit(solution)/shard_map/ppermute | solution.py:24
  130.5 19.0 %collective-permute-start.4 = (f32[3,3,3,3,4,1,128]{6,4,5,3,2,1,0:T(4,128)S(1)}, f32[3,3,3,3,4,1,128]{6,4,5,3,2,1,0:T(4,128)S(1)}, u32[]{:S(2)}, u32[]{:S(2)}) collective-permute-start(f32[3,3,3,3,4,1,128]{6,4,5,3,2,1,0:T(4,128)S(1)} %get-tuple-element.76), channel_id=1, source_target_pairs={{0,1},{1,2},{2,3},{3,4},{4,5},{5,6},{6,7},{7,0},{8,9},{9,10},{10,1... | collective-permute-start | bytes 497672 | tf_op jit(solution)/shard_map/ppermute | solution.py:21
  136.1 15.8 %collective-permute-start.5 = (f32[3,3,3,3,4,1,128]{6,4,5,3,2,1,0:T(4,128)S(1)}, f32[3,3,3,3,4,1,128]{6,4,5,3,2,1,0:T(4,128)S(1)}, u32[]{:S(2)}, u32[]{:S(2)}) collective-permute-start(f32[3,3,3,3,4,1,128]{6,4,5,3,2,1,0:T(4,128)S(1)} %get-tuple-element.77), channel_id=1, source_target_pairs={{1,0},{2,1},{3,2},{4,3},{5,4},{6,5},{7,6},{0,7},{9,8},{10,9},{11,1... | collective-permute-start | bytes 497672 | tf_op jit(solution)/shard_map/ppermute | solution.py:24
  154.7 10.4 %collective-permute-start.6 = (f32[3,3,3,3,1,8,128]{6,5,4,3,2,1,0:T(8,128)S(1)}, f32[3,3,3,3,1,8,128]{6,5,4,3,2,1,0:T(8,128)S(1)}, u32[]{:S(2)}, u32[]{:S(2)}) collective-permute-start(f32[3,3,3,3,1,8,128]{6,5,4,3,2,1,0:T(8,128)S(1)} %get-tuple-element.233), channel_id=1, source_target_pairs={{0,8},{8,16},{16,24},{24,32},{32,40},{40,48},{48,56},{56,64},{64,7... | collective-permute-start | bytes 995336 | tf_op jit(solution)/shard_map/ppermute | solution.py:21
  161.0 11.0 %collective-permute-start.7 = (f32[3,3,3,3,1,8,128]{6,5,4,3,2,1,0:T(8,128)S(1)}, f32[3,3,3,3,1,8,128]{6,5,4,3,2,1,0:T(8,128)S(1)}, u32[]{:S(2)}, u32[]{:S(2)}) collective-permute-start(f32[3,3,3,3,1,8,128]{6,5,4,3,2,1,0:T(8,128)S(1)} %get-tuple-element.234), channel_id=1, source_target_pairs={{8,0},{16,8},{24,16},{32,24},{40,32},{48,40},{56,48},{64,56},{72,6... | collective-permute-start | bytes 995336 | tf_op jit(solution)/shard_map/ppermute | solution.py:24
  172.2 11.2 %collective-permute-start.9 = (f32[3,3,3,3,4,1,128]{6,4,5,3,2,1,0:T(4,128)S(1)}, f32[3,3,3,3,4,1,128]{6,4,5,3,2,1,0:T(4,128)S(1)}, u32[]{:S(2)}, u32[]{:S(2)}) collective-permute-start(f32[3,3,3,3,4,1,128]{6,4,5,3,2,1,0:T(4,128)S(1)} %bitcast.91), channel_id=1, source_target_pairs={{1,0},{2,1},{3,2},{4,3},{5,4},{6,5},{7,6},{0,7},{9,8},{10,9},{11,1... | collective-permute-start | bytes 497672 | tf_op jit(solution)/shard_map/ppermute | solution.py:24
  177.8 15.3 %collective-permute-start.8 = (f32[3,3,3,3,4,1,128]{6,4,5,3,2,1,0:T(4,128)S(1)}, f32[3,3,3,3,4,1,128]{6,4,5,3,2,1,0:T(4,128)S(1)}, u32[]{:S(2)}, u32[]{:S(2)}) collective-permute-start(f32[3,3,3,3,4,1,128]{6,4,5,3,2,1,0:T(4,128)S(1)} %bitcast.83), channel_id=1, source_target_pairs={{0,1},{1,2},{2,3},{3,4},{4,5},{5,6},{6,7},{7,0},{8,9},{9,10},{10,1... | collective-permute-start | bytes 497672 | tf_op jit(solution)/shard_map/ppermute | solution.py:21
  194.2 10.6 %collective-permute-start.10 = (f32[3,3,3,3,1,8,128]{6,5,4,3,2,1,0:T(8,128)S(1)}, f32[3,3,3,3,1,8,128]{6,5,4,3,2,1,0:T(8,128)S(1)}, u32[]{:S(2)}, u32[]{:S(2)}) collective-permute-start(f32[3,3,3,3,1,8,128]{6,5,4,3,2,1,0:T(8,128)S(1)} %get-tuple-element.223), channel_id=1, source_target_pairs={{0,8},{8,16},{16,24},{24,32},{32,40},{40,48},{48,56},{56,64},{64,7... | collective-permute-start | bytes 995336 | tf_op jit(solution)/shard_map/ppermute | solution.py:21
  209.4 12.2 %collective-permute-start.13 = (f32[3,3,3,3,4,1,128]{6,4,5,3,2,1,0:T(4,128)S(1)}, f32[3,3,3,3,4,1,128]{6,4,5,3,2,1,0:T(4,128)S(1)}, u32[]{:S(2)}, u32[]{:S(2)}) collective-permute-start(f32[3,3,3,3,4,1,128]{6,4,5,3,2,1,0:T(4,128)S(1)} %bitcast.92), channel_id=1, source_target_pairs={{1,0},{2,1},{3,2},{4,3},{5,4},{6,5},{7,6},{0,7},{9,8},{10,9},{11,1... | collective-permute-start | bytes 497672 | tf_op jit(solution)/shard_map/ppermute | solution.py:24
  213.1 14.8 %collective-permute-start.12 = (f32[3,3,3,3,4,1,128]{6,4,5,3,2,1,0:T(4,128)S(1)}, f32[3,3,3,3,4,1,128]{6,4,5,3,2,1,0:T(4,128)S(1)}, u32[]{:S(2)}, u32[]{:S(2)}) collective-permute-start(f32[3,3,3,3,4,1,128]{6,4,5,3,2,1,0:T(4,128)S(1)} %bitcast.84), channel_id=1, source_target_pairs={{0,1},{1,2},{2,3},{3,4},{4,5},{5,6},{6,7},{7,0},{8,9},{9,10},{10,1... | collective-permute-start | bytes 497672 | tf_op jit(solution)/shard_map/ppermute | solution.py:21
  229.1 9.6 %collective-permute-start.14 = (f32[3,3,3,3,1,8,128]{6,5,4,3,2,1,0:T(8,128)S(1)}, f32[3,3,3,3,1,8,128]{6,5,4,3,2,1,0:T(8,128)S(1)}, u32[]{:S(2)}, u32[]{:S(2)}) collective-permute-start(f32[3,3,3,3,1,8,128]{6,5,4,3,2,1,0:T(8,128)S(1)} %get-tuple-element.213), channel_id=1, source_target_pairs={{0,8},{8,16},{16,24},{24,32},{32,40},{40,48},{48,56},{56,64},{64,7... | collective-permute-start | bytes 995336 | tf_op jit(solution)/shard_map/ppermute | solution.py:21
  234.7 11.2 %collective-permute-start.15 = (f32[3,3,3,3,1,8,128]{6,5,4,3,2,1,0:T(8,128)S(1)}, f32[3,3,3,3,1,8,128]{6,5,4,3,2,1,0:T(8,128)S(1)}, u32[]{:S(2)}, u32[]{:S(2)}) collective-permute-start(f32[3,3,3,3,1,8,128]{6,5,4,3,2,1,0:T(8,128)S(1)} %get-tuple-element.214), channel_id=1, source_target_pairs={{8,0},{16,8},{24,16},{32,24},{40,32},{48,40},{56,48},{64,56},{72,6... | collective-permute-start | bytes 995336 | tf_op jit(solution)/shard_map/ppermute | solution.py:24
  246.1 13.2 %collective-permute-start.17 = (f32[3,3,3,3,4,1,128]{6,4,5,3,2,1,0:T(4,128)S(1)}, f32[3,3,3,3,4,1,128]{6,4,5,3,2,1,0:T(4,128)S(1)}, u32[]{:S(2)}, u32[]{:S(2)}) collective-permute-start(f32[3,3,3,3,4,1,128]{6,4,5,3,2,1,0:T(4,128)S(1)} %bitcast.96), channel_id=1, source_target_pairs={{1,0},{2,1},{3,2},{4,3},{5,4},{6,5},{7,6},{0,7},{9,8},{10,9},{11,1... | collective-permute-start | bytes 497672 | tf_op jit(solution)/shard_map/ppermute | solution.py:24
  248.0 15.4 %collective-permute-start.16 = (f32[3,3,3,3,4,1,128]{6,4,5,3,2,1,0:T(4,128)S(1)}, f32[3,3,3,3,4,1,128]{6,4,5,3,2,1,0:T(4,128)S(1)}, u32[]{:S(2)}, u32[]{:S(2)}) collective-permute-start(f32[3,3,3,3,4,1,128]{6,4,5,3,2,1,0:T(4,128)S(1)} %bitcast.89), channel_id=1, source_target_pairs={{0,1},{1,2},{2,3},{3,4},{4,5},{5,6},{6,7},{7,0},{8,9},{9,10},{10,1... | collective-permute-start | bytes 497672 | tf_op jit(solution)/shard_map/ppermute | solution.py:21
  267.6 12.5 %collective-permute-start.19 = (f32[3,3,3,3,1,8,128]{6,5,4,3,2,1,0:T(8,128)S(1)}, f32[3,3,3,3,1,8,128]{6,5,4,3,2,1,0:T(8,128)S(1)}, u32[]{:S(2)}, u32[]{:S(2)}) collective-permute-start(f32[3,3,3,3,1,8,128]{6,5,4,3,2,1,0:T(8,128)S(1)} %get-tuple-element.204), channel_id=1, source_target_pairs={{8,0},{16,8},{24,16},{32,24},{40,32},{48,40},{56,48},{64,56},{72,6... | collective-permute-start | bytes 995336 | tf_op jit(solution)/shard_map/ppermute | solution.py:24
  280.2 13.8 %collective-permute-start.21 = (f32[3,3,3,3,4,1,128]{6,4,5,3,2,1,0:T(4,128)S(1)}, f32[3,3,3,3,4,1,128]{6,4,5,3,2,1,0:T(4,128)S(1)}, u32[]{:S(2)}, u32[]{:S(2)}) collective-permute-start(f32[3,3,3,3,4,1,128]{6,4,5,3,2,1,0:T(4,128)S(1)} %bitcast.93), channel_id=1, source_target_pairs={{1,0},{2,1},{3,2},{4,3},{5,4},{6,5},{7,6},{0,7},{9,8},{10,9},{11,1... | collective-permute-start | bytes 497672 | tf_op jit(solution)/shard_map/ppermute | solution.py:24
  285.8 19.2 %collective-permute-start.20 = (f32[3,3,3,3,4,1,128]{6,4,5,3,2,1,0:T(4,128)S(1)}, f32[3,3,3,3,4,1,128]{6,4,5,3,2,1,0:T(4,128)S(1)}, u32[]{:S(2)}, u32[]{:S(2)}) collective-permute-start(f32[3,3,3,3,4,1,128]{6,4,5,3,2,1,0:T(4,128)S(1)} %bitcast.85), channel_id=1, source_target_pairs={{0,1},{1,2},{2,3},{3,4},{4,5},{5,6},{6,7},{7,0},{8,9},{9,10},{10,1... | collective-permute-start | bytes 497672 | tf_op jit(solution)/shard_map/ppermute | solution.py:21
  308.2 12.2 %collective-permute-start.23 = (f32[3,3,3,3,1,8,128]{6,5,4,3,2,1,0:T(8,128)S(1)}, f32[3,3,3,3,1,8,128]{6,5,4,3,2,1,0:T(8,128)S(1)}, u32[]{:S(2)}, u32[]{:S(2)}) collective-permute-start(f32[3,3,3,3,1,8,128]{6,5,4,3,2,1,0:T(8,128)S(1)} %get-tuple-element.194), channel_id=1, source_target_pairs={{8,0},{16,8},{24,16},{32,24},{40,32},{48,40},{56,48},{64,56},{72,6... | collective-permute-start | bytes 995336 | tf_op jit(solution)/shard_map/ppermute | solution.py:24
  320.7 18.5 %collective-permute-start.25 = (f32[3,3,3,3,4,1,128]{6,4,5,3,2,1,0:T(4,128)S(1)}, f32[3,3,3,3,4,1,128]{6,4,5,3,2,1,0:T(4,128)S(1)}, u32[]{:S(2)}, u32[]{:S(2)}) collective-permute-start(f32[3,3,3,3,4,1,128]{6,4,5,3,2,1,0:T(4,128)S(1)} %bitcast.94), channel_id=1, source_target_pairs={{1,0},{2,1},{3,2},{4,3},{5,4},{6,5},{7,6},{0,7},{9,8},{10,9},{11,1... | collective-permute-start | bytes 497672 | tf_op jit(solution)/shard_map/ppermute | solution.py:24
  325.7 13.8 %collective-permute-start.24 = (f32[3,3,3,3,4,1,128]{6,4,5,3,2,1,0:T(4,128)S(1)}, f32[3,3,3,3,4,1,128]{6,4,5,3,2,1,0:T(4,128)S(1)}, u32[]{:S(2)}, u32[]{:S(2)}) collective-permute-start(f32[3,3,3,3,4,1,128]{6,4,5,3,2,1,0:T(4,128)S(1)} %bitcast.86), channel_id=1, source_target_pairs={{0,1},{1,2},{2,3},{3,4},{4,5},{5,6},{6,7},{7,0},{8,9},{9,10},{10,1... | collective-permute-start | bytes 497672 | tf_op jit(solution)/shard_map/ppermute | solution.py:21
  340.8 11.2 %collective-permute-start.26 = (f32[3,3,3,3,1,8,128]{6,5,4,3,2,1,0:T(8,128)S(1)}, f32[3,3,3,3,1,8,128]{6,5,4,3,2,1,0:T(8,128)S(1)}, u32[]{:S(2)}, u32[]{:S(2)}) collective-permute-start(f32[3,3,3,3,1,8,128]{6,5,4,3,2,1,0:T(8,128)S(1)} %get-tuple-element.183), channel_id=1, source_target_pairs={{0,8},{8,16},{16,24},{24,32},{32,40},{40,48},{48,56},{56,64},{64,7... | collective-permute-start | bytes 995336 | tf_op jit(solution)/shard_map/ppermute | solution.py:21
  357.1 15.3 %collective-permute-start.29 = (f32[3,3,3,3,4,1,128]{6,4,5,3,2,1,0:T(4,128)S(1)}, f32[3,3,3,3,4,1,128]{6,4,5,3,2,1,0:T(4,128)S(1)}, u32[]{:S(2)}, u32[]{:S(2)}) collective-permute-start(f32[3,3,3,3,4,1,128]{6,4,5,3,2,1,0:T(4,128)S(1)} %bitcast.97), channel_id=1, source_target_pairs={{1,0},{2,1},{3,2},{4,3},{5,4},{6,5},{7,6},{0,7},{9,8},{10,9},{11,1... | collective-permute-start | bytes 497672 | tf_op jit(solution)/shard_map/ppermute | solution.py:24
  360.0 14.0 %collective-permute-start.28 = (f32[3,3,3,3,4,1,128]{6,4,5,3,2,1,0:T(4,128)S(1)}, f32[3,3,3,3,4,1,128]{6,4,5,3,2,1,0:T(4,128)S(1)}, u32[]{:S(2)}, u32[]{:S(2)}) collective-permute-start(f32[3,3,3,3,4,1,128]{6,4,5,3,2,1,0:T(4,128)S(1)} %bitcast.90), channel_id=1, source_target_pairs={{0,1},{1,2},{2,3},{3,4},{4,5},{5,6},{6,7},{7,0},{8,9},{9,10},{10,1... | collective-permute-start | bytes 497672 | tf_op jit(solution)/shard_map/ppermute | solution.py:21
  381.6 12.1 %collective-permute-start.31 = (f32[3,3,3,3,1,8,128]{6,5,4,3,2,1,0:T(8,128)S(1)}, f32[3,3,3,3,1,8,128]{6,5,4,3,2,1,0:T(8,128)S(1)}, u32[]{:S(2)}, u32[]{:S(2)}) collective-permute-start(f32[3,3,3,3,1,8,128]{6,5,4,3,2,1,0:T(8,128)S(1)} %get-tuple-element.174), channel_id=1, source_target_pairs={{8,0},{16,8},{24,16},{32,24},{40,32},{48,40},{56,48},{64,56},{72,6... | collective-permute-start | bytes 995336 | tf_op jit(solution)/shard_map/ppermute | solution.py:24
  393.9 12.2 %collective-permute-start.33 = (f32[3,3,3,3,4,1,128]{6,4,5,3,2,1,0:T(4,128)S(1)}, f32[3,3,3,3,4,1,128]{6,4,5,3,2,1,0:T(4,128)S(1)}, u32[]{:S(2)}, u32[]{:S(2)}) collective-permute-start(f32[3,3,3,3,4,1,128]{6,4,5,3,2,1,0:T(4,128)S(1)} %bitcast.95), channel_id=1, source_target_pairs={{1,0},{2,1},{3,2},{4,3},{5,4},{6,5},{7,6},{0,7},{9,8},{10,9},{11,1... | collective-permute-start | bytes 497672 | tf_op jit(solution)/shard_map/ppermute | solution.py:24
  400.7 12.1 %collective-permute-start.32 = (f32[3,3,3,3,4,1,128]{6,4,5,3,2,1,0:T(4,128)S(1)}, f32[3,3,3,3,4,1,128]{6,4,5,3,2,1,0:T(4,128)S(1)}, u32[]{:S(2)}, u32[]{:S(2)}) collective-permute-start(f32[3,3,3,3,4,1,128]{6,4,5,3,2,1,0:T(4,128)S(1)} %bitcast.87), channel_id=1, source_target_pairs={{0,1},{1,2},{2,3},{3,4},{4,5},{5,6},{6,7},{7,0},{8,9},{9,10},{10,1... | collective-permute-start | bytes 497672 | tf_op jit(solution)/shard_map/ppermute | solution.py:21
  419.6 9.9 %collective-permute-start.35 = (f32[3,3,3,3,1,8,128]{6,5,4,3,2,1,0:T(8,128)S(1)}, f32[3,3,3,3,1,8,128]{6,5,4,3,2,1,0:T(8,128)S(1)}, u32[]{:S(2)}, u32[]{:S(2)}) collective-permute-start(f32[3,3,3,3,1,8,128]{6,5,4,3,2,1,0:T(8,128)S(1)} %get-tuple-element.164), channel_id=1, source_target_pairs={{8,0},{16,8},{24,16},{32,24},{40,32},{48,40},{56,48},{64,56},{72,6... | collective-permute-start | bytes 995336 | tf_op jit(solution)/shard_map/ppermute | solution.py:24
  429.6 12.9 %collective-permute-start.37 = (f32[3,3,3,3,4,1,128]{6,4,5,3,2,1,0:T(4,128)S(1)}, f32[3,3,3,3,4,1,128]{6,4,5,3,2,1,0:T(4,128)S(1)}, u32[]{:S(2)}, u32[]{:S(2)}) collective-permute-start(f32[3,3,3,3,4,1,128]{6,4,5,3,2,1,0:T(4,128)S(1)} %bitcast.88), channel_id=1, source_target_pairs={{1,0},{2,1},{3,2},{4,3},{5,4},{6,5},{7,6},{0,7},{9,8},{10,9},{11,1... | collective-permute-start | bytes 497672 | tf_op jit(solution)/shard_map/ppermute | solution.py:24
  433.0 17.8 %collective-permute-start.36 = (f32[3,3,3,3,4,1,128]{6,4,5,3,2,1,0:T(4,128)S(1)}, f32[3,3,3,3,4,1,128]{6,4,5,3,2,1,0:T(4,128)S(1)}, u32[]{:S(2)}, u32[]{:S(2)}) collective-permute-start(f32[3,3,3,3,4,1,128]{6,4,5,3,2,1,0:T(4,128)S(1)} %bitcast.82), channel_id=1, source_target_pairs={{0,1},{1,2},{2,3},{3,4},{4,5},{5,6},{6,7},{7,0},{8,9},{9,10},{10,1... | collective-permute-start | bytes 497672 | tf_op jit(solution)/shard_map/ppermute | solution.py:21
  (10 other events, 95.6 us)
where the time goes:
time: 454 us; the launch traced here: 453 us
  starting transfers between devices  171 us (38%)
  waiting for transfers between devices  154 us (34%)
  blocking collectives  97.2 us (21%)
  other arithmetic  19.3 us (4%)
  local copies, waits for them, and re-layouts  9.28 us (2%)
    pmax x1, blocking collectives, on_device(): fastest = lax.pmax(local_fast, ('slab', 'sub'))  97.2 us
    ppermute x18, waiting for transfers between devices, extended(): lax.ppermute(lax.slice_in_dim(block, 0, width, axis=dim), axis, backward)  88.7 us
    ppermute x18, starting transfers between devices, extended(): lax.ppermute(lax.slice_in_dim(block, block.shape[dim] - width, None, axis...  87.8 us
    ppermute x18, starting transfers between devices, extended(): lax.ppermute(lax.slice_in_dim(block, 0, width, axis=dim), axis, backward)  69.4 us
    ppermute x18, waiting for transfers between devices, extended(): lax.ppermute(lax.slice_in_dim(block, block.shape[dim] - width, None, axis...  65.6 us
    ppermute x2, starting transfers between devices, from_behind(): lax.ppermute(array, axis, [(i, (i + by) % length) for i in range(length)])  13.4 us
  transfers between devices with their start and end apart: 38, of which 33 were waited for; matrix products, arithmetic and copies ran while one was open for 2% of the time, Pallas kernels for 0%

commit v1 on v0

v1 whole, which is shorter than its diff:
```python
import functools

import jax
import jax.numpy as jnp
from jax import lax
from jax.experimental import pallas as pl
from jax.experimental.pallas import tpu as pltpu
from jax.sharding import PartitionSpec as P

STEPS = 3
STAGES = 3 * STEPS
FIELDS = 3
ROWS = 2
COURANT = 0.12
SOFTNESS = 0.05
NODE_WEIGHTS = (1.0, 4.0, 1.0)
MESH = pl.DeviceIdType.MESH
X_TILES = 11
Y_ROWS = 24


def line_terms(v0, v1, v2, a, flux_lo, flux_hi):
    d = v2 - v0
    t = (v0 + v2) + 4.0 * v1
    big = a * t
    small = a * d
    twice = small + small
    return (big - twice) + flux_lo, small, -((big + twice) + flux_hi)


def kernel(
    n_slab,
    n_sub,
    fields_hbm,
    speeds_hbm,
    out_hbm,
    state,
    speeds,
    bounds,
    coef,
    send_x,
    recv_x,
    send_y,
    recv_y,
    speed_send,
    speed_recv_x,
    speed_recv_y,
    near_max,
    far_max,
    max_send,
    load_sem,
    store_sem,
    face_send_sem,
    face_recv_sem,
    speed_send_sem,
    speed_recv_sem,
    max_send_sem,
    max_recv_sem,
):
    slab = lax.axis_index("slab")
    sub = lax.axis_index("sub")
    n_near, n_far = near_max.shape[0], far_max.shape[0]
    near_at = lax.rem(sub, 2) * 8 + lax.rem(slab, 8)
    far_at = lax.div(slab, 8) * (n_sub // 2) + lax.div(sub, 2)

    def next_along(axis, by):
        size = {"slab": n_slab, "sub": n_sub}[axis]
        return {axis: lax.rem(lax.axis_index(axis) + (by + size), size)}

    def near_device(by):
        at = lax.rem(near_at + by, n_near)
        return {
            "slab": lax.div(slab, 8) * 8 + lax.rem(at, 8),
            "sub": lax.div(sub, 2) * 2 + lax.div(at, 8),
        }

    def far_device(by):
        at = lax.rem(far_at + by, n_far)
        return {
            "slab": lax.div(at, n_sub // 2) * 8 + lax.rem(slab, 8),
            "sub": lax.rem(at, n_sub // 2) * 2 + lax.rem(sub, 2),
        }

    load_speeds = pltpu.make_async_copy(speeds_hbm, speeds, load_sem.at[FIELDS])
    load_speeds.start()
    loads = []
    for f in range(FIELDS):
        load = pltpu.make_async_copy(fields_hbm.at[f], state.at[0, f], load_sem.at[f])
        load.start()
        loads.append(load)

    barrier = pltpu.get_barrier_semaphore()
    greeted = [next_along(axis, by) for axis in ("sub", "slab") for by in (1, -1)]
    greeted += [far_device(by) for by in range(1, n_far)]
    greeted += [near_device(by) for by in range(1, n_near)]
    for device in greeted:
        pl.semaphore_signal(barrier, inc=1, device_id=device, device_id_type=MESH)
    load_speeds.wait()
    for r in range(ROWS):
        speed_send[r : r + 1, :] = speeds[1, r, 0:1, :]
    pl.semaphore_wait(barrier, len(greeted))

    speed_y = pltpu.make_async_remote_copy(
        src_ref=speed_send,
        dst_ref=speed_recv_y,
        send_sem=speed_send_sem.at[0],
        recv_sem=speed_recv_sem.at[0],
        device_id=next_along("sub", -1),
        device_id_type=MESH,
    )
    speed_x = pltpu.make_async_remote_copy(
        src_ref=speeds.at[0, 0],
        dst_ref=speed_recv_x,
        send_sem=speed_send_sem.at[1],
        recv_sem=speed_recv_sem.at[1],
        device_id=next_along("slab", -1),
        device_id_type=MESH,
    )
    speed_y.start()
    speed_x.start()

    def face_copies(t, f):
        copies = []
        for axis, sent, received in (("sub", send_y, recv_y), ("slab", send_x, recv_x)):
            for way, by in ((0, 1), (1, -1)):
                at = (0 if axis == "sub" else 2) + way
                copies.append(
                    pltpu.make_async_remote_copy(
                        src_ref=sent.at[t, f, way],
                        dst_ref=received.at[t, f, way],
                        send_sem=face_send_sem.at[t, f, at],
                        recv_sem=face_recv_sem.at[t, f, at],
                        device_id=next_along(axis, by),
                        device_id_type=MESH,
                    )
                )
        return copies

    def pack_faces(t, f, r, values):
        for i in range(3):
            for j in range(3):
                for k in range(3):
                    v = values[i][j][k]
                    if i == 2 and r == ROWS - 1:
                        send_x[t, f, 0, 3 * j + k] = v
                    if i == 0 and r == 0:
                        send_x[t, f, 1, 3 * j + k] = v
                    at = 9 * r + 3 * i + k
                    if j == 2:
                        send_y[t, f, 0, at : at + 1, :] = v[7:8, :]
                    if j == 0:
                        send_y[t, f, 1, at : at + 1, :] = v[0:1, :]

    def pack_bounds(t, f, r, lowest, highest):
        for n, v in ((0, lowest), (1, highest)):
            bounds[f, r, n] = v
            if r == ROWS - 1:
                send_x[t, f, 0, 9 + n] = v
            if r == 0:
                send_x[t, f, 1, 9 + n] = v
            at = 18 + 2 * r + n
            send_y[t, f, 0, at : at + 1, :] = v[7:8, :]
            send_y[t, f, 1, at : at + 1, :] = v[0:1, :]

    def first_faces(f, _):
        for r in range(ROWS):
            values = [
                [[state[0, f, i, j, k, r] for k in range(3)] for j in range(3)] for i in range(3)
            ]
            flat = [values[i][j][k] for i in range(3) for j in range(3) for k in range(3)]
            pack_faces(0, f, r, values)
            pack_bounds(
                0, f, r, functools.reduce(jnp.minimum, flat), functools.reduce(jnp.maximum, flat)
            )
        for copy in face_copies(0, f):
            copy.start()
        return 0

    for load in loads:
        load.wait()
    lax.fori_loop(0, FIELDS, first_faces, 0)

    row_at = lax.broadcasted_iota(jnp.int32, (8, 128), 0)
    at_bottom = row_at == 0
    at_top = row_at == 7

    speed_y.wait_recv()
    speed_x.wait_recv()
    face_x = [speeds[0, r] for r in range(ROWS)] + [speed_recv_x[...]]
    y_lo = [speeds[1, r] for r in range(ROWS)]
    y_hi = [
        jnp.where(
            at_top,
            jnp.broadcast_to(speed_recv_y[r : r + 1, :], (8, 128)),
            pltpu.roll(y_lo[r], 7, 0),
        )
        for r in range(ROWS)
    ]
    z_lo = [speeds[2, r] for r in range(ROWS)]
    interiors = [
        [0.5 * (face_x[r] + face_x[r + 1]) for r in range(ROWS)],
        [0.5 * (y_lo[r] + y_hi[r]) for r in range(ROWS)],
        [0.5 * (z_lo[r] + pltpu.roll(z_lo[r], 127, 1)) for r in range(ROWS)],
    ]
    fast = None
    for r in range(ROWS):
        total = jnp.abs(interiors[0][r]) + jnp.abs(interiors[1][r]) + jnp.abs(interiors[2][r])
        fast = total if fast is None else jnp.maximum(fast, total)
    fast = jnp.max(fast, axis=0, keepdims=True)
    max_copies = []
    for phase, (received, device_of) in enumerate(((near_max, near_device), (far_max, far_device))):
        n = received.shape[0]
        received[0] = fast
        if n > 1:
            max_send[phase] = fast
            for by in range(1, n):
                copy = pltpu.make_async_remote_copy(
                    src_ref=max_send.at[phase],
                    dst_ref=received.at[by],
                    send_sem=max_send_sem.at[phase],
                    recv_sem=max_recv_sem.at[phase],
                    device_id=device_of(by),
                    device_id_type=MESH,
                )
                copy.start()
            pltpu.make_async_copy(
                received.at[pl.ds(1, n - 1)], received.at[pl.ds(1, n - 1)], max_recv_sem.at[phase]
            ).wait()
            fast = jnp.max(received[...], axis=0)
    fastest = jnp.max(jnp.broadcast_to(fast, (8, 128)), axis=1, keepdims=True)
    time_step = COURANT / (jnp.broadcast_to(fastest, (8, 128)) + 1e-6)
    six = 6.0 * time_step
    up = lambda s: six * jnp.maximum(s, 0.0)
    down = lambda s: six * jnp.minimum(s, 0.0)
    for r in range(ROWS):
        for d in range(3):
            coef[3 * r + d] = -(time_step * interiors[d][r])
        for n, v in enumerate(
            (up(y_lo[r]), down(y_lo[r]), up(y_hi[r]), down(y_hi[r]), up(z_lo[r]), down(z_lo[r]))
        ):
            coef[6 + 6 * r + n] = v
    for q in range(ROWS + 1):
        coef[18 + 2 * q] = up(face_x[q])
        coef[19 + 2 * q] = down(face_x[q])

    def stage(n, _):
        t = lax.div(n, FIELDS)
        f = lax.rem(n, FIELDS)
        part = lax.rem(t, 3)
        source = part
        target = lax.rem(part + 1, 3)
        share = jnp.where(part == 0, 0.0, jnp.where(part == 1, 0.75, 1.0 / 3.0)).astype(jnp.float32)
        rest = jnp.where(part == 0, 1.0, jnp.where(part == 1, 0.25, 2.0 / 3.0)).astype(jnp.float32)
        for copy in face_copies(t, f):
            copy.wait_recv()

        @pl.when(part == 0)
        def _():
            low = [bounds[f, r, 0] for r in range(ROWS)]
            high = [bounds[f, r, 1] for r in range(ROWS)]
            for values, at, pick in ((low, 0, jnp.minimum), (high, 1, jnp.maximum)):
                ring = [recv_x[t, f, 0, 9 + at]] + values + [recv_x[t, f, 1, 9 + at]]
                for r in range(ROWS):
                    here = 18 + 2 * r + at
                    v = values[r]
                    below = jnp.where(
                        at_bottom,
                        jnp.broadcast_to(recv_y[t, f, 0, here : here + 1, :], (8, 128)),
                        pltpu.roll(v, 1, 0),
                    )
                    above = jnp.where(
                        at_top,
                        jnp.broadcast_to(recv_y[t, f, 1, here : here + 1, :], (8, 128)),
                        pltpu.roll(v, 7, 0),
                    )
                    best = pick(pick(v, ring[r]), ring[r + 2])
                    best = pick(best, pick(below, above))
                    best = pick(best, pick(pltpu.roll(v, 1, 1), pltpu.roll(v, 127, 1)))
                    bounds[f, r, 2 + at] = best

        for r in range(ROWS):
            v = [
                [[state[source, f, i, j, k, r] for k in range(3)] for j in range(3)]
                for i in range(3)
            ]
            new = [[[v[i][j][k] for k in range(3)] for j in range(3)] for i in range(3)]
            a = [coef[3 * r + d] for d in range(3)]
            up_x = [coef[18 + 2 * q] for q in (r, r + 1)]
            down_x = [coef[19 + 2 * q] for q in (r, r + 1)]
            up_y, down_y, up_y_hi, down_y_hi, up_z, down_z = [coef[6 + 6 * r + n] for n in range(6)]
            for k in range(3):
                for j in range(3):
                    at = 3 * j + k
                    if r == 0:
                        before = recv_x[t, f, 0, at]
                    else:
                        before = state[source, f, 2, j, k, r - 1]
                    if r == ROWS - 1:
                        after = recv_x[t, f, 1, at]
                    else:
                        after = state[source, f, 0, j, k, r + 1]
                    flux_lo = up_x[0] * before + down_x[0] * v[0][j][k]
                    flux_hi = up_x[1] * v[2][j][k] + down_x[1] * after
                    terms = line_terms(v[0][j][k], v[1][j][k], v[2][j][k], a[0], flux_lo, flux_hi)
                    for i in range(3):
                        new[i][j][k] = new[i][j][k] + terms[i]
                for i in range(3):
                    at = 9 * r + 3 * i + k
                    before = jnp.where(
                        at_bottom,
                        jnp.broadcast_to(recv_y[t, f, 0, at : at + 1, :], (8, 128)),
                        pltpu.roll(v[i][2][k], 1, 0),
                    )
                    after = jnp.where(
                        at_top,
                        jnp.broadcast_to(recv_y[t, f, 1, at : at + 1, :], (8, 128)),
                        pltpu.roll(v[i][0][k], 7, 0),
                    )
                    flux_lo = up_y * before + down_y * v[i][0][k]
                    flux_hi = up_y_hi * v[i][2][k] + down_y_hi * after
                    terms = line_terms(v[i][0][k], v[i][1][k], v[i][2][k], a[1], flux_lo, flux_hi)
                    for j in range(3):
                        new[i][j][k] = new[i][j][k] + terms[j]
            average = largest = smallest = None
            for i in range(3):
                for j in range(3):
                    flux_lo = up_z * pltpu.roll(v[i][j][2], 1, 1) + down_z * v[i][j][0]
                    flux_hi = pltpu.roll(flux_lo, 127, 1)
                    terms = line_terms(v[i][j][0], v[i][j][1], v[i][j][2], a[2], flux_lo, flux_hi)
                    for k in range(3):
                        x = share * state[0, f, i, j, k, r] + rest * (new[i][j][k] + terms[k])
                        new[i][j][k] = x
                        largest = x if largest is None else jnp.maximum(largest, x)
                        smallest = x if smallest is None else jnp.minimum(smallest, x)
                    line = (new[i][j][0] + new[i][j][2]) + 4.0 * new[i][j][1]
                    weight = NODE_WEIGHTS[i] * NODE_WEIGHTS[j]
                    line = line if weight == 1.0 else weight * line
                    average = line if average is None else average + line
            average = average * (1.0 / 216.0)
            lowest = bounds[f, r, 2]
            highest = bounds[f, r, 3]
            upper = (jnp.maximum(highest - average, 0.0) + SOFTNESS) / (largest - average + SOFTNESS)
            lower = (jnp.maximum(average - lowest, 0.0) + SOFTNESS) / (average - smallest + SOFTNESS)
            scaling = jnp.minimum(1.0, jnp.minimum(upper, lower))
            offset = average - scaling * average
            for i in range(3):
                for j in range(3):
                    for k in range(3):
                        x = scaling * new[i][j][k] + offset
                        new[i][j][k] = x
                        state[target, f, i, j, k, r] = x

            @pl.when(t < STAGES - 1)
            def _():
                pack_faces(t + 1, f, r, new)
                pack_bounds(t + 1, f, r, scaling * smallest + offset, scaling * largest + offset)

        @pl.when(t < STAGES - 1)
        def _():
            for copy in face_copies(t + 1, f):
                copy.start()

        @pl.when(t == STAGES - 1)
        def _():
            pltpu.make_async_copy(state.at[0, f], out_hbm.at[f], store_sem.at[f]).start()

        return 0

    lax.fori_loop(0, STAGES * FIELDS, stage, 0)

    speed_y.wait_send()
    speed_x.wait_send()
    for phase, received in enumerate((near_max, far_max)):
        n = received.shape[0]
        if n > 1:
            pltpu.make_async_copy(
                received.at[pl.ds(1, n - 1)], received.at[pl.ds(1, n - 1)], max_send_sem.at[phase]
            ).wait()

    def drain(n, _):
        for copy in face_copies(lax.div(n, FIELDS), lax.rem(n, FIELDS)):
            copy.wait_send()
        return 0

    lax.fori_loop(0, STAGES * FIELDS, drain, 0)
    for f in range(FIELDS):
        pltpu.make_async_copy(state.at[0, f], out_hbm.at[f], store_sem.at[f]).wait()


def solution(mesh):
    n_slab, n_sub = mesh.shape["slab"], mesh.shape["sub"]
    n_near = 16
    n_far = n_slab * n_sub // n_near

    def on_device(fields, speeds):
        vmem = lambda *shape: pltpu.VMEM(shape, jnp.float32)
        dma = lambda *shape: pltpu.SemaphoreType.DMA(shape)
        return pl.pallas_call(
            functools.partial(kernel, n_slab, n_sub),
            out_shape=jax.ShapeDtypeStruct(fields.shape, fields.dtype),
            in_specs=[pl.BlockSpec(memory_space=pl.ANY)] * 2,
            out_specs=pl.BlockSpec(memory_space=pl.ANY),
            scratch_shapes=[
                vmem(3, FIELDS, 3, 3, 3, ROWS, 8, 128),
                vmem(3, ROWS, 8, 128),
                vmem(FIELDS, ROWS, 4, 8, 128),
                vmem(24, 8, 128),
                vmem(STAGES, FIELDS, 2, X_TILES, 8, 128),
                vmem(STAGES, FIELDS, 2, X_TILES, 8, 128),
                vmem(STAGES, FIELDS, 2, Y_ROWS, 128),
                vmem(STAGES, FIELDS, 2, Y_ROWS, 128),
                vmem(8, 128),
                vmem(8, 128),
                vmem(8, 128),
                vmem(n_near, 1, 128),
                vmem(n_far, 1, 128),
                vmem(2, 1, 128),
                dma(FIELDS + 1),
                dma(FIELDS),
                dma(STAGES, FIELDS, 4),
                dma(STAGES, FIELDS, 4),
                dma(2),
                dma(2),
                dma(2),
                dma(2),
            ],
            compiler_params=pltpu.CompilerParams(
                collective_id=1, has_side_effects=True, vmem_limit_bytes=48 * 1024 * 1024
            ),
            name="remap",
        )(fields, speeds)

    spec = P(None, None, None, None, "slab", "sub", None)
    return jax.shard_map(
        on_device,
        mesh=mesh,
        in_specs=(spec, P(None, "slab", "sub", None)),
        out_specs=spec,
        check_vma=False,
    )
```

time: 454 us -> 95 us (0.21)
  starting transfers between devices: 171 us -> 0 us
  waiting for transfers between devices: 154 us -> 0 us
  blocking collectives: 97.2 us -> 0 us
  Pallas kernels: 0 us -> 91.2 us
  other arithmetic: 19.3 us -> 0 us
  local copies, waits for them, and re-layouts: 9.28 us -> 2.67 us
    ppermute x38 -> x0, starting transfers between devices: 171 us -> none  [the longest x18 87.8 us: extended(): lax.ppermute(lax.slice_in_dim(block, block.shape[dim] - width, None, axis...]
    ppermute x38 -> x0, waiting for transfers between devices: 154 us -> none  [the longest x18 88.7 us: extended(): lax.ppermute(lax.slice_in_dim(block, 0, width, axis=dim), axis, backward)]
    pmax x1 -> x0, blocking collectives: 97.2 us -> none  [on_device(): fastest = lax.pmax(local_fast, ('slab', 'sub'))]
    pallas_call x0 -> x1, Pallas kernels: none -> 91.2 us  [on_device(): pl.pallas_call(functools.partial(kernel, n_slab, n_sub), out_shape=jax.Sh...]
    mul x28 -> x0, other arithmetic: 8.48 us -> none  [the longest x27 8.41 us: direction_term(): outputs.append(-2.0 * contrib)]
    slice x101 -> x0, local copies, waits for them, and re-layouts: 6.98 us -> none  [the longest x9 2.32 us: extended(): lax.slice_in_dim(block, block.shape[dim] - width, None, axis=dim)]
    reduce_max x12 -> x0, other arithmetic: 6.05 us -> none  [the longest x9 3.37 us: limiter(): largest = jnp.max(values, axis=(1, 2, 3), keepdims=True)]
  transfers between devices with their start and end apart: 38 -> 0, of which waited for: 33 -> 0; matrix products, arithmetic and copies ran while one was open for 2% -> 0% of each run, Pallas kernels for 0% -> 0%
where the time goes in v1:
time: 95 us; the launch traced here: 93.9 us
  Pallas kernels  91.2 us (96%)
  local copies, waits for them, and re-layouts  2.67 us (3%)
    pallas_call x1, Pallas kernels, on_device(): pl.pallas_call(functools.partial(kernel, n_slab, n_sub), out_shape=jax.Sh...  91.2 us
    unnamed x5, local copies, waits for them, and re-layouts  2.67 us

profile of v1, /device:TPU:1, one launch (start us, length us, event | category | flops | bytes accessed | tf_op | source)
XLA Modules:
  0.0 93.9 jit_solution(18048911700698942723)
XLA Ops:
  0.0 0.0 copy-start
  0.0 1.1 %copy-done = f32[3,3,3,3,2,8,128]{6,5,4,3,2,1,0:T(8,128)S(1)} copy-done((f32[3,3,3,3,2,8,128]{6,5,4,3,2,1,0:T(8,128)S(1)}, f32[3,3,3,3,2,8,128]{6,5,4,3,2,1,0:T(8,128)}, u32[]{:S(2)}) %copy-start) | copy-done | bytes 663576
  1.1 0.0 copy-start.1
  1.1 0.7 copy-done.1
  1.8 91.2 %remap.1 = f32[3,3,3,3,2,8,128]{6,5,4,3,2,1,0:T(8,128)S(1)} custom-call(f32[3,3,3,3,2,8,128]{6,5,4,3,2,1,0:T(8,128)S(1)} %copy-done, f32[3,2,8,128]{3,2,1,0:T(8,128)S(1)} %copy-done.1), custom_call_target="tpu_custom_call" | custom-call | tf_op jit(solution)/shard_map/remap/pallas_call | solution.py:398
  93.0 0.8 copy.4
Async XLA Ops:
  0.0 1.1 %copy-start = (f32[3,3,3,3,2,8,128]{6,5,4,3,2,1,0:T(8,128)S(1)}, f32[3,3,3,3,2,8,128]{6,5,4,3,2,1,0:T(8,128)}, u32[]{:S(2)}) copy-start(f32[3,3,3,3,2,8,128]{6,5,4,3,2,1,0:T(8,128)} %fields_hbm.1) | copy-start | bytes 1990660
  1.1 0.7 copy-start.1

commit v2 on v1

--- a/solution.py
+++ b/solution.py
@@ -15,8 +15,17 @@
 SOFTNESS = 0.05
 NODE_WEIGHTS = (1.0, 4.0, 1.0)
 MESH = pl.DeviceIdType.MESH
-X_TILES = 11
-Y_ROWS = 24
+X_TILES, X_NODES = 11, 9
+Y_ROWS, Y_USED, Y_NODES = 24, 22, 18
+
+
+def tree(pick, values):
+    while len(values) > 1:
+        values = [
+            pick(values[n], values[n + 1]) if n + 1 < len(values) else values[n]
+            for n in range(0, len(values), 2)
+        ]
+    return values[0]
 
 
 def line_terms(v0, v1, v2, a, flux_lo, flux_hi):
@@ -35,6 +44,7 @@
     speeds_hbm,
     out_hbm,
     state,
+    partial,
     speeds,
     bounds,
     coef,
@@ -119,15 +129,18 @@
     speed_y.start()
     speed_x.start()
 
-    def face_copies(t, f):
+    def face_copies(t, f, with_bounds):
         copies = []
-        for axis, sent, received in (("sub", send_y, recv_y), ("slab", send_x, recv_x)):
+        for axis, sent, received, size in (
+            ("sub", send_y, recv_y, Y_USED if with_bounds else Y_NODES),
+            ("slab", send_x, recv_x, X_TILES if with_bounds else X_NODES),
+        ):
             for way, by in ((0, 1), (1, -1)):
                 at = (0 if axis == "sub" else 2) + way
                 copies.append(
                     pltpu.make_async_remote_copy(
-                        src_ref=sent.at[t, f, way],
-                        dst_ref=received.at[t, f, way],
+                        src_ref=sent.at[t, f, way, pl.ds(0, size)],
+                        dst_ref=received.at[t, f, way, pl.ds(0, size)],
                         send_sem=face_send_sem.at[t, f, at],
                         recv_sem=face_recv_sem.at[t, f, at],
                         device_id=next_along(axis, by),
@@ -135,6 +148,17 @@
                     )
                 )
         return copies
+
+    def for_faces(t, f, action):
+        @pl.when(lax.rem(t, 3) == 0)
+        def _():
+            for copy in face_copies(t, f, True):
+                action(copy)
+
+        @pl.when(lax.rem(t, 3) != 0)
+        def _():
+            for copy in face_copies(t, f, False):
+                action(copy)
 
     def pack_faces(t, f, r, values):
         for i in range(3):
@@ -170,9 +194,9 @@
             flat = [values[i][j][k] for i in range(3) for j in range(3) for k in range(3)]
             pack_faces(0, f, r, values)
             pack_bounds(
-                0, f, r, functools.reduce(jnp.minimum, flat), functools.reduce(jnp.maximum, flat)
+                0, f, r, tree(jnp.minimum, flat), tree(jnp.maximum, flat)
             )
-        for copy in face_copies(0, f):
+        for copy in face_copies(0, f, True):
             copy.start()
         return 0
 
@@ -235,49 +259,34 @@
     for r in range(ROWS):
         for d in range(3):
             coef[3 * r + d] = -(time_step * interiors[d][r])
+        y_up, y_down = up(y_lo[r]), down(y_hi[r])
         for n, v in enumerate(
-            (up(y_lo[r]), down(y_lo[r]), up(y_hi[r]), down(y_hi[r]), up(z_lo[r]), down(z_lo[r]))
+            (
+                jnp.where(at_bottom, 0.0, y_up),
+                down(y_lo[r]),
+                up(y_hi[r]),
+                jnp.where(at_top, 0.0, y_down),
+                up(z_lo[r]),
+                down(z_lo[r]),
+                jnp.where(at_bottom, y_up, 0.0),
+                jnp.where(at_top, y_down, 0.0),
+            )
         ):
-            coef[6 + 6 * r + n] = v
+            coef[6 + 8 * r + n] = v
     for q in range(ROWS + 1):
-        coef[18 + 2 * q] = up(face_x[q])
-        coef[19 + 2 * q] = down(face_x[q])
-
-    def stage(n, _):
-        t = lax.div(n, FIELDS)
-        f = lax.rem(n, FIELDS)
+        coef[22 + 2 * q] = up(face_x[q])
+        coef[23 + 2 * q] = down(face_x[q])
+
+    def shares(t):
         part = lax.rem(t, 3)
-        source = part
-        target = lax.rem(part + 1, 3)
-        share = jnp.where(part == 0, 0.0, jnp.where(part == 1, 0.75, 1.0 / 3.0)).astype(jnp.float32)
-        rest = jnp.where(part == 0, 1.0, jnp.where(part == 1, 0.25, 2.0 / 3.0)).astype(jnp.float32)
-        for copy in face_copies(t, f):
-            copy.wait_recv()
-
-        @pl.when(part == 0)
-        def _():
-            low = [bounds[f, r, 0] for r in range(ROWS)]
-            high = [bounds[f, r, 1] for r in range(ROWS)]
-            for values, at, pick in ((low, 0, jnp.minimum), (high, 1, jnp.maximum)):
-                ring = [recv_x[t, f, 0, 9 + at]] + values + [recv_x[t, f, 1, 9 + at]]
-                for r in range(ROWS):
-                    here = 18 + 2 * r + at
-                    v = values[r]
-                    below = jnp.where(
-                        at_bottom,
-                        jnp.broadcast_to(recv_y[t, f, 0, here : here + 1, :], (8, 128)),
-                        pltpu.roll(v, 1, 0),
-                    )
-                    above = jnp.where(
-                        at_top,
-                        jnp.broadcast_to(recv_y[t, f, 1, here : here + 1, :], (8, 128)),
-                        pltpu.roll(v, 7, 0),
-                    )
-                    best = pick(pick(v, ring[r]), ring[r + 2])
-                    best = pick(best, pick(below, above))
-                    best = pick(best, pick(pltpu.roll(v, 1, 1), pltpu.roll(v, 127, 1)))
-                    bounds[f, r, 2 + at] = best
-
+        pick = lambda *values: jnp.where(
+            part == 0, values[0], jnp.where(part == 1, values[1], values[2])
+        ).astype(jnp.float32)
+        return pick(0.0, 0.75, 1.0 / 3.0), pick(1.0, 0.25, 2.0 / 3.0)
+
+    def inner_part(t, f):
+        source = lax.rem(t, 3)
+        share, rest = shares(t)
         for r in range(ROWS):
             v = [
                 [[state[source, f, i, j, k, r] for k in range(3)] for j in range(3)]
@@ -285,58 +294,89 @@
             ]
             new = [[[v[i][j][k] for k in range(3)] for j in range(3)] for i in range(3)]
             a = [coef[3 * r + d] for d in range(3)]
-            up_x = [coef[18 + 2 * q] for q in (r, r + 1)]
-            down_x = [coef[19 + 2 * q] for q in (r, r + 1)]
-            up_y, down_y, up_y_hi, down_y_hi, up_z, down_z = [coef[6 + 6 * r + n] for n in range(6)]
+            up_x = [coef[22 + 2 * q] for q in (r, r + 1)]
+            down_x = [coef[23 + 2 * q] for q in (r, r + 1)]
+            up_y, down_y, up_y_hi, down_y_hi, up_z, down_z = [coef[6 + 8 * r + n] for n in range(6)]
             for k in range(3):
                 for j in range(3):
-                    at = 3 * j + k
-                    if r == 0:
-                        before = recv_x[t, f, 0, at]
-                    else:
-                        before = state[source, f, 2, j, k, r - 1]
-                    if r == ROWS - 1:
-                        after = recv_x[t, f, 1, at]
-                    else:
-                        after = state[source, f, 0, j, k, r + 1]
-                    flux_lo = up_x[0] * before + down_x[0] * v[0][j][k]
-                    flux_hi = up_x[1] * v[2][j][k] + down_x[1] * after
+                    flux_lo = down_x[0] * v[0][j][k]
+                    if r > 0:
+                        flux_lo = flux_lo + up_x[0] * state[source, f, 2, j, k, r - 1]
+                    flux_hi = up_x[1] * v[2][j][k]
+                    if r < ROWS - 1:
+                        flux_hi = flux_hi + down_x[1] * state[source, f, 0, j, k, r + 1]
                     terms = line_terms(v[0][j][k], v[1][j][k], v[2][j][k], a[0], flux_lo, flux_hi)
                     for i in range(3):
                         new[i][j][k] = new[i][j][k] + terms[i]
                 for i in range(3):
-                    at = 9 * r + 3 * i + k
-                    before = jnp.where(
-                        at_bottom,
-                        jnp.broadcast_to(recv_y[t, f, 0, at : at + 1, :], (8, 128)),
-                        pltpu.roll(v[i][2][k], 1, 0),
-                    )
-                    after = jnp.where(
-                        at_top,
-                        jnp.broadcast_to(recv_y[t, f, 1, at : at + 1, :], (8, 128)),
-                        pltpu.roll(v[i][0][k], 7, 0),
-                    )
-                    flux_lo = up_y * before + down_y * v[i][0][k]
-                    flux_hi = up_y_hi * v[i][2][k] + down_y_hi * after
+                    flux_lo = up_y * pltpu.roll(v[i][2][k], 1, 0) + down_y * v[i][0][k]
+                    flux_hi = up_y_hi * v[i][2][k] + down_y_hi * pltpu.roll(v[i][0][k], 7, 0)
                     terms = line_terms(v[i][0][k], v[i][1][k], v[i][2][k], a[1], flux_lo, flux_hi)
                     for j in range(3):
                         new[i][j][k] = new[i][j][k] + terms[j]
-            average = largest = smallest = None
             for i in range(3):
                 for j in range(3):
                     flux_lo = up_z * pltpu.roll(v[i][j][2], 1, 1) + down_z * v[i][j][0]
                     flux_hi = pltpu.roll(flux_lo, 127, 1)
                     terms = line_terms(v[i][j][0], v[i][j][1], v[i][j][2], a[2], flux_lo, flux_hi)
                     for k in range(3):
-                        x = share * state[0, f, i, j, k, r] + rest * (new[i][j][k] + terms[k])
-                        new[i][j][k] = x
-                        largest = x if largest is None else jnp.maximum(largest, x)
-                        smallest = x if smallest is None else jnp.minimum(smallest, x)
-                    line = (new[i][j][0] + new[i][j][2]) + 4.0 * new[i][j][1]
+                        partial[f, i, j, k, r] = share * state[0, f, i, j, k, r] + rest * (
+                            new[i][j][k] + terms[k]
+                        )
+
+    def spread(row):
+        return jnp.broadcast_to(row, (8, 128))
+
+    def gather_bounds(t, f):
+        for at, pick in ((0, jnp.minimum), (1, jnp.maximum)):
+            values = [bounds[f, r, at] for r in range(ROWS)]
+            ring = [recv_x[t, f, 0, 9 + at]] + values + [recv_x[t, f, 1, 9 + at]]
+            for r in range(ROWS):
+                here = 18 + 2 * r + at
+                v = values[r]
+                below = jnp.where(
+                    at_bottom, spread(recv_y[t, f, 0, here : here + 1, :]), pltpu.roll(v, 1, 0)
+                )
+                above = jnp.where(
+                    at_top, spread(recv_y[t, f, 1, here : here + 1, :]), pltpu.roll(v, 7, 0)
+                )
+                best = pick(pick(v, ring[r]), ring[r + 2])
+                best = pick(best, pick(below, above))
+                best = pick(best, pick(pltpu.roll(v, 1, 1), pltpu.roll(v, 127, 1)))
+                bounds[f, r, 2 + at] = best
+
+    def outer_part(t, f):
+        target = lax.rem(t + 1, 3)
+        _, rest = shares(t)
+        for r in range(ROWS):
+            x = [
+                [[partial[f, i, j, k, r] for k in range(3)] for j in range(3)] for i in range(3)
+            ]
+            up_y, down_y = [rest * coef[12 + 8 * r + n] for n in range(2)]
+            for k in range(3):
+                for j in range(3):
+                    if r == 0:
+                        up_x = rest * coef[22]
+                        x[0][j][k] = x[0][j][k] + up_x * recv_x[t, f, 0, 3 * j + k]
+                    if r == ROWS - 1:
+                        down_x = rest * coef[23 + 2 * ROWS]
+                        x[2][j][k] = x[2][j][k] - down_x * recv_x[t, f, 1, 3 * j + k]
+                for i in range(3):
+                    at = 9 * r + 3 * i + k
+                    x[i][0][k] = x[i][0][k] + up_y * spread(recv_y[t, f, 0, at : at + 1, :])
+                    x[i][2][k] = x[i][2][k] - down_y * spread(recv_y[t, f, 1, at : at + 1, :])
+            averages, tops, bottoms = [], [], []
+            for i in range(3):
+                for j in range(3):
+                    lo, mid, hi = x[i][j]
+                    tops.append(jnp.maximum(jnp.maximum(lo, hi), mid))
+                    bottoms.append(jnp.minimum(jnp.minimum(lo, hi), mid))
+                    line = (lo + hi) + 4.0 * mid
                     weight = NODE_WEIGHTS[i] * NODE_WEIGHTS[j]
-                    line = line if weight == 1.0 else weight * line
-                    average = line if average is None else average + line
-            average = average * (1.0 / 216.0)
+                    averages.append(line if weight == 1.0 else weight * line)
+            average = tree(jnp.add, averages) * (1.0 / 216.0)
+            largest = tree(jnp.maximum, tops)
+            smallest = tree(jnp.minimum, bottoms)
             lowest = bounds[f, r, 2]
             highest = bounds[f, r, 3]
             upper = (jnp.maximum(highest - average, 0.0) + SOFTNESS) / (largest - average + SOFTNESS)
@@ -346,19 +386,31 @@
             for i in range(3):
                 for j in range(3):
                     for k in range(3):
-                        x = scaling * new[i][j][k] + offset
-                        new[i][j][k] = x
-                        state[target, f, i, j, k, r] = x
-
-            @pl.when(t < STAGES - 1)
-            def _():
-                pack_faces(t + 1, f, r, new)
-                pack_bounds(t + 1, f, r, scaling * smallest + offset, scaling * largest + offset)
+                        x[i][j][k] = scaling * x[i][j][k] + offset
+                        state[target, f, i, j, k, r] = x[i][j][k]
+            pack_faces(t + 1, f, r, x)
+            pack_bounds(t + 1, f, r, scaling * smallest + offset, scaling * largest + offset)
+
+    def stage(n, _):
+        t = lax.div(n, FIELDS)
+        f = lax.rem(n, FIELDS)
+
+        @pl.when(t == 0)
+        def _():
+            inner_part(0, f)
+
+        for_faces(t, f, lambda copy: copy.wait_recv())
+
+        @pl.when(lax.rem(t, 3) == 0)
+        def _():
+            gather_bounds(t, f)
+
+        outer_part(t, f)
 
         @pl.when(t < STAGES - 1)
         def _():
-            for copy in face_copies(t + 1, f):
-                copy.start()
+            for_faces(t + 1, f, lambda copy: copy.start())
+            inner_part(t + 1, f)
 
         @pl.when(t == STAGES - 1)
         def _():
@@ -378,8 +430,7 @@
             ).wait()
 
     def drain(n, _):
-        for copy in face_copies(lax.div(n, FIELDS), lax.rem(n, FIELDS)):
-            copy.wait_send()
+        for_faces(lax.div(n, FIELDS), lax.rem(n, FIELDS), lambda copy: copy.wait_send())
         return 0
 
     lax.fori_loop(0, STAGES * FIELDS, drain, 0)
@@ -398,16 +449,17 @@
         return pl.pallas_call(
             functools.partial(kernel, n_slab, n_sub),
             out_shape=jax.ShapeDtypeStruct(fields.shape, fields.dtype),
-            in_specs=[pl.BlockSpec(memory_space=pl.ANY)] * 2,
+            in_specs=[pl.BlockSpec(memory_space=pltpu.HBM)] * 2,
             out_specs=pl.BlockSpec(memory_space=pl.ANY),
             scratch_shapes=[
                 vmem(3, FIELDS, 3, 3, 3, ROWS, 8, 128),
+                vmem(FIELDS, 3, 3, 3, ROWS, 8, 128),
                 vmem(3, ROWS, 8, 128),
                 vmem(FIELDS, ROWS, 4, 8, 128),
-                vmem(24, 8, 128),
+                vmem(24 + 2 * ROWS, 8, 128),
+                vmem(STAGES + 1, FIELDS, 2, X_TILES, 8, 128),
                 vmem(STAGES, FIELDS, 2, X_TILES, 8, 128),
-                vmem(STAGES, FIELDS, 2, X_TILES, 8, 128),
-                vmem(STAGES, FIELDS, 2, Y_ROWS, 128),
+                vmem(STAGES + 1, FIELDS, 2, Y_ROWS, 128),
                 vmem(STAGES, FIELDS, 2, Y_ROWS, 128),
                 vmem(8, 128),
                 vmem(8, 128),
@@ -425,7 +477,7 @@
                 dma(2),
             ],
             compiler_params=pltpu.CompilerParams(
-                collective_id=1, has_side_effects=True, vmem_limit_bytes=48 * 1024 * 1024
+                collective_id=1, has_side_effects=True, vmem_limit_bytes=60 * 1024 * 1024
             ),
             name="remap",
         )(fields, speeds)

time: 95 us -> 89.2 us (0.939)
  Pallas kernels: 91.2 us -> 85.9 us
    pallas_call x1, Pallas kernels: 91.2 us -> 85.9 us  [on_device(): pl.pallas_call(functools.partial(kernel, n_slab, n_sub), out_shape=jax.Sh...]
    unnamed x5 -> x1, local copies, waits for them, and re-layouts: 2.67 us -> 1.97 us
where the time goes in v2:
time: 89.2 us; the launch traced here: 87.8 us
  Pallas kernels  85.9 us (96%)
  local copies, waits for them, and re-layouts  1.97 us (2%)
    pallas_call x1, Pallas kernels, on_device(): pl.pallas_call(functools.partial(kernel, n_slab, n_sub), out_shape=jax.Sh...  85.9 us
    unnamed x1, local copies, waits for them, and re-layouts  1.97 us

profile of v2, /device:TPU:1, one launch (start us, length us, event | category | flops | bytes accessed | tf_op | source)
XLA Modules:
  0.0 87.8 jit_solution(17980418511121144575)
XLA Ops:
  0.0 85.9 %remap.1 = f32[3,3,3,3,2,8,128]{6,5,4,3,2,1,0:T(8,128)} custom-call(f32[3,3,3,3,2,8,128]{6,5,4,3,2,1,0:T(8,128)} %fields_hbm.1, f32[3,2,8,128]{3,2,1,0:T(8,128)} %speeds_hbm.1), custom_call_target="tpu_custom_call" | custom-call | tf_op jit(solution)/shard_map/remap/pallas_call | solution.py:449
  85.9 2.0 %copy.4 = f32[3,3,3,3,2,8,128]{6,5,4,3,2,1,0:T(8,128)} copy(f32[3,3,3,3,2,8,128]{6,5,4,3,2,1,0:T(8,128)} %remap.1) | data formatting | bytes 1327104

commit v3 on v2

v3 whole, which is shorter than its diff:
```python
import functools

import jax
import jax.numpy as jnp
from jax import lax
from jax.experimental import pallas as pl
from jax.experimental.pallas import tpu as pltpu
from jax.sharding import PartitionSpec as P

STEPS = 3
STAGES = 3 * STEPS
FIELDS = 3
ROWS = 2
COURANT = 0.12
SOFTNESS = 0.05
NODE_WEIGHTS = (1.0, 4.0, 1.0)
MESH = pl.DeviceIdType.MESH
X_TILES, X_NODES = 11, 9
Y_ROWS, Y_USED, Y_NODES = 24, 22, 18


def ring_distance(by, size):
    return min(by, size - by)


def farthest_first(outer, inner, hops):
    steps = [(a, b) for a in range(outer) for b in range(inner) if a or b]
    return sorted(steps, key=lambda step: -hops(*step))


def tree(pick, values):
    while len(values) > 1:
        values = [
            pick(values[n], values[n + 1]) if n + 1 < len(values) else values[n]
            for n in range(0, len(values), 2)
        ]
    return values[0]


def line_terms(v0, v1, v2, a, flux_lo, flux_hi):
    d = v2 - v0
    t = (v0 + v2) + 4.0 * v1
    big = a * t
    small = a * d
    twice = small + small
    return (big - twice) + flux_lo, small, -((big + twice) + flux_hi)


def kernel(
    n_slab,
    n_sub,
    fields_hbm,
    speeds_hbm,
    out_hbm,
    state,
    partial,
    speeds,
    bounds,
    coef,
    send_x,
    recv_x,
    send_y,
    recv_y,
    speed_send,
    speed_recv_x,
    speed_recv_y,
    near_max,
    far_max,
    max_send,
    load_sem,
    store_sem,
    face_send_sem,
    face_recv_sem,
    speed_send_sem,
    speed_recv_sem,
    max_send_sem,
    max_recv_sem,
):
    slab = lax.axis_index("slab")
    sub = lax.axis_index("sub")
    n_z, n_x = n_slab // 8, n_sub // 2

    def shifted(at, by, size):
        moved = at + by
        return jnp.where(moved >= size, moved - size, moved)

    z, l = lax.div(slab, 8), lax.rem(slab, 8)
    x, h = lax.div(sub, 2), lax.rem(sub, 2)
    along_l = [8 * z + shifted(l, by, 8) for by in range(8)]
    along_h = [2 * x + shifted(h, by, 2) for by in range(2)]
    along_z = [8 * shifted(z, by, n_z) + l for by in range(n_z)]
    along_x = [2 * shifted(x, by, n_x) + h for by in range(n_x)]
    near = [
        (2 * by_l + by_h, {"slab": along_l[by_l], "sub": along_h[by_h]})
        for by_h, by_l in farthest_first(
            2, 8, lambda by_h, by_l: ring_distance((4 * by_h + by_l // 2) % 8, 8)
        )
    ]
    far = [
        (n_x * by_z + by_x, {"slab": along_z[by_z], "sub": along_x[by_x]})
        for by_z, by_x in farthest_first(
            n_z, n_x, lambda by_z, by_x: ring_distance(by_z, n_z) + ring_distance(by_x, n_x)
        )
    ]
    neighbours = []
    for axis, at, size, odd in (("sub", sub, n_sub, h), ("slab", slab, n_slab, lax.rem(l, 2))):
        after = shifted(at, 1, size)
        before = shifted(at, size - 1, size)
        neighbours.append((axis, 1 - odd, {axis: jnp.where(odd == 1, after, before)}))
        neighbours.append((axis, odd, {axis: jnp.where(odd == 1, before, after)}))
    previous = {"sub": {"sub": shifted(sub, n_sub - 1, n_sub)}, "slab": {"slab": shifted(slab, n_slab - 1, n_slab)}}

    load_speeds = pltpu.make_async_copy(speeds_hbm, speeds, load_sem.at[FIELDS])
    load_speeds.start()
    loads = []
    for f in range(FIELDS):
        load = pltpu.make_async_copy(fields_hbm.at[f], state.at[0, f], load_sem.at[f])
        load.start()
        loads.append(load)

    barrier = pltpu.get_barrier_semaphore()
    greeted = [device for _, _, device in neighbours] + [device for _, device in far + near]
    for device in greeted:
        pl.semaphore_signal(barrier, inc=1, device_id=device, device_id_type=MESH)
    load_speeds.wait()
    for r in range(ROWS):
        speed_send[r : r + 1, :] = speeds[1, r, 0:1, :]
    pl.semaphore_wait(barrier, len(greeted))

    speed_y = pltpu.make_async_remote_copy(
        src_ref=speed_send,
        dst_ref=speed_recv_y,
        send_sem=speed_send_sem.at[0],
        recv_sem=speed_recv_sem.at[0],
        device_id=previous["sub"],
        device_id_type=MESH,
    )
    speed_x = pltpu.make_async_remote_copy(
        src_ref=speeds.at[0, 0],
        dst_ref=speed_recv_x,
        send_sem=speed_send_sem.at[1],
        recv_sem=speed_recv_sem.at[1],
        device_id=previous["slab"],
        device_id_type=MESH,
    )
    speed_y.start()
    speed_x.start()

    def face_copies(n, with_bounds):
        copies = []
        for slot, (axis, way, device) in enumerate(neighbours):
            if axis == "sub":
                sent, received, size = send_y, recv_y, Y_USED if with_bounds else Y_NODES
            else:
                sent, received, size = send_x, recv_x, X_TILES if with_bounds else X_NODES
            copies.append(
                pltpu.make_async_remote_copy(
                    src_ref=sent.at[n, way, pl.ds(0, size)],
                    dst_ref=received.at[n, way, pl.ds(0, size)],
                    send_sem=face_send_sem.at[n, slot],
                    recv_sem=face_recv_sem.at[n, slot],
                    device_id=device,
                    device_id_type=MESH,
                )
            )
        return copies

    def for_faces(n, part, action):
        @pl.when(part == 0)
        def _():
            for copy in face_copies(n, True):
                action(copy)

        @pl.when(part != 0)
        def _():
            for copy in face_copies(n, False):
                action(copy)

    def pack_faces(n, r, values):
        for i in range(3):
            for j in range(3):
                for k in range(3):
                    v = values[i][j][k]
                    if i == 2 and r == ROWS - 1:
                        send_x[n, 0, 3 * j + k] = v
                    if i == 0 and r == 0:
                        send_x[n, 1, 3 * j + k] = v
                    at = 9 * r + 3 * i + k
                    if j == 2:
                        send_y[n, 0, at : at + 1, :] = v[7:8, :]
                    if j == 0:
                        send_y[n, 1, at : at + 1, :] = v[0:1, :]

    def pack_bounds(n, f, r, lowest, highest):
        for which, v in ((0, lowest), (1, highest)):
            bounds[f, r, which] = v
            if r == ROWS - 1:
                send_x[n, 0, 9 + which] = v
            if r == 0:
                send_x[n, 1, 9 + which] = v
            at = 18 + 2 * r + which
            send_y[n, 0, at : at + 1, :] = v[7:8, :]
            send_y[n, 1, at : at + 1, :] = v[0:1, :]

    def first_faces(f, _):
        for r in range(ROWS):
            values = [
                [[state[0, f, i, j, k, r] for k in range(3)] for j in range(3)] for i in range(3)
            ]
            flat = [values[i][j][k] for i in range(3) for j in range(3) for k in range(3)]
            pack_faces(f, r, values)
            pack_bounds(
                f, f, r, tree(jnp.minimum, flat), tree(jnp.maximum, flat)
            )
        for copy in face_copies(f, True):
            copy.start()
        return 0

    for load in loads:
        load.wait()
    lax.fori_loop(0, FIELDS, first_faces, 0)

    row_at = lax.broadcasted_iota(jnp.int32, (8, 128), 0)
    at_bottom = row_at == 0
    at_top = row_at == 7

    speed_y.wait_recv()
    speed_x.wait_recv()
    face_x = [speeds[0, r] for r in range(ROWS)] + [speed_recv_x[...]]
    y_lo = [speeds[1, r] for r in range(ROWS)]
    y_hi = [
        jnp.where(
            at_top,
            jnp.broadcast_to(speed_recv_y[r : r + 1, :], (8, 128)),
            pltpu.roll(y_lo[r], 7, 0),
        )
        for r in range(ROWS)
    ]
    z_lo = [speeds[2, r] for r in range(ROWS)]
    interiors = [
        [0.5 * (face_x[r] + face_x[r + 1]) for r in range(ROWS)],
        [0.5 * (y_lo[r] + y_hi[r]) for r in range(ROWS)],
        [0.5 * (z_lo[r] + pltpu.roll(z_lo[r], 127, 1)) for r in range(ROWS)],
    ]
    fast = None
    for r in range(ROWS):
        total = jnp.abs(interiors[0][r]) + jnp.abs(interiors[1][r]) + jnp.abs(interiors[2][r])
        fast = total if fast is None else jnp.maximum(fast, total)
    fast = jnp.max(fast, axis=0, keepdims=True)
    def coefficients():
        up = lambda s: 6.0 * jnp.maximum(s, 0.0)
        down = lambda s: 6.0 * jnp.minimum(s, 0.0)
        tiles = [-interiors[d][r] for r in range(ROWS) for d in range(3)]
        for r in range(ROWS):
            y_up, y_down = up(y_lo[r]), down(y_hi[r])
            tiles += [
                jnp.where(at_bottom, 0.0, y_up),
                down(y_lo[r]),
                up(y_hi[r]),
                jnp.where(at_top, 0.0, y_down),
                up(z_lo[r]),
                down(z_lo[r]),
                jnp.where(at_bottom, y_up, 0.0),
                jnp.where(at_top, y_down, 0.0),
            ]
        for q in range(ROWS + 1):
            tiles += [up(face_x[q]), down(face_x[q])]
        return tiles

    def shares(t):
        part = lax.rem(t, 3)
        pick = lambda *values: jnp.where(
            part == 0, values[0], jnp.where(part == 1, values[1], values[2])
        ).astype(jnp.float32)
        return pick(0.0, 0.75, 1.0 / 3.0), pick(1.0, 0.25, 2.0 / 3.0)

    def inner_part(t, f, rate_only=False):
        source = lax.rem(t, 3)
        share, rest = shares(t)
        for r in range(ROWS):
            v = [
                [[state[source, f, i, j, k, r] for k in range(3)] for j in range(3)]
                for i in range(3)
            ]
            new = [
                [[None if rate_only else v[i][j][k] for k in range(3)] for j in range(3)]
                for i in range(3)
            ]
            a = [coef[3 * r + d] for d in range(3)]
            up_x = [coef[22 + 2 * q] for q in (r, r + 1)]
            down_x = [coef[23 + 2 * q] for q in (r, r + 1)]
            up_y, down_y, up_y_hi, down_y_hi, up_z, down_z = [coef[6 + 8 * r + n] for n in range(6)]
            for k in range(3):
                for j in range(3):
                    flux_lo = down_x[0] * v[0][j][k]
                    if r > 0:
                        flux_lo = flux_lo + up_x[0] * state[source, f, 2, j, k, r - 1]
                    flux_hi = up_x[1] * v[2][j][k]
                    if r < ROWS - 1:
                        flux_hi = flux_hi + down_x[1] * state[source, f, 0, j, k, r + 1]
                    terms = line_terms(v[0][j][k], v[1][j][k], v[2][j][k], a[0], flux_lo, flux_hi)
                    for i in range(3):
                        new[i][j][k] = terms[i] if rate_only else new[i][j][k] + terms[i]
                for i in range(3):
                    flux_lo = up_y * pltpu.roll(v[i][2][k], 1, 0) + down_y * v[i][0][k]
                    flux_hi = up_y_hi * v[i][2][k] + down_y_hi * pltpu.roll(v[i][0][k], 7, 0)
                    terms = line_terms(v[i][0][k], v[i][1][k], v[i][2][k], a[1], flux_lo, flux_hi)
                    for j in range(3):
                        new[i][j][k] = new[i][j][k] + terms[j]
            for i in range(3):
                for j in range(3):
                    flux_lo = up_z * pltpu.roll(v[i][j][2], 1, 1) + down_z * v[i][j][0]
                    flux_hi = pltpu.roll(flux_lo, 127, 1)
                    terms = line_terms(v[i][j][0], v[i][j][1], v[i][j][2], a[2], flux_lo, flux_hi)
                    for k in range(3):
                        x = new[i][j][k] + terms[k]
                        if not rate_only:
                            x = share * state[0, f, i, j, k, r] + rest * x
                        partial[f, i, j, k, r] = x

    for phase, (received, partners) in enumerate(((near_max, near), (far_max, far))):
        n = received.shape[0]
        received[0] = fast
        if n > 1:
            max_send[phase] = fast
            for slot, device in partners:
                copy = pltpu.make_async_remote_copy(
                    src_ref=max_send.at[phase],
                    dst_ref=received.at[slot],
                    send_sem=max_send_sem.at[phase],
                    recv_sem=max_recv_sem.at[phase],
                    device_id=device,
                    device_id_type=MESH,
                )
                copy.start()
            if phase == 0:
                for at, v in enumerate(coefficients()):
                    coef[at] = v
                lax.fori_loop(0, FIELDS, lambda f, _: (inner_part(0, f, True), 0)[1], 0)
            pltpu.make_async_copy(
                received.at[pl.ds(1, n - 1)], received.at[pl.ds(1, n - 1)], max_recv_sem.at[phase]
            ).wait()
            fast = jnp.max(received[...], axis=0)
    fastest = jnp.max(jnp.broadcast_to(fast, (8, 128)), axis=1, keepdims=True)
    time_step = COURANT / (jnp.broadcast_to(fastest, (8, 128)) + 1e-6)
    for at in range(coef.shape[0]):
        coef[at] = time_step * coef[at]

    def begin(f):
        for r in range(ROWS):
            for i in range(3):
                for j in range(3):
                    for k in range(3):
                        at = (f, i, j, k, r)
                        partial[at] = state[(0, *at)] + time_step * partial[at]

    def spread(row):
        return jnp.broadcast_to(row, (8, 128))

    def gather_bounds(n, f):
        for at, pick in ((0, jnp.minimum), (1, jnp.maximum)):
            values = [bounds[f, r, at] for r in range(ROWS)]
            ring = [recv_x[n, 0, 9 + at]] + values + [recv_x[n, 1, 9 + at]]
            for r in range(ROWS):
                here = 18 + 2 * r + at
                v = values[r]
                below = jnp.where(
                    at_bottom, spread(recv_y[n, 0, here : here + 1, :]), pltpu.roll(v, 1, 0)
                )
                above = jnp.where(
                    at_top, spread(recv_y[n, 1, here : here + 1, :]), pltpu.roll(v, 7, 0)
                )
                best = pick(pick(v, ring[r]), ring[r + 2])
                best = pick(best, pick(below, above))
                best = pick(best, pick(pltpu.roll(v, 1, 1), pltpu.roll(v, 127, 1)))
                bounds[f, r, 2 + at] = best

    def outer_part(n, t, f):
        target = lax.rem(t + 1, 3)
        _, rest = shares(t)
        for r in range(ROWS):
            x = [
                [[partial[f, i, j, k, r] for k in range(3)] for j in range(3)] for i in range(3)
            ]
            up_y, down_y = [rest * coef[12 + 8 * r + n] for n in range(2)]
            for k in range(3):
                for j in range(3):
                    if r == 0:
                        up_x = rest * coef[22]
                        x[0][j][k] = x[0][j][k] + up_x * recv_x[n, 0, 3 * j + k]
                    if r == ROWS - 1:
                        down_x = rest * coef[23 + 2 * ROWS]
                        x[2][j][k] = x[2][j][k] - down_x * recv_x[n, 1, 3 * j + k]
                for i in range(3):
                    at = 9 * r + 3 * i + k
                    x[i][0][k] = x[i][0][k] + up_y * spread(recv_y[n, 0, at : at + 1, :])
                    x[i][2][k] = x[i][2][k] - down_y * spread(recv_y[n, 1, at : at + 1, :])
            averages, tops, bottoms = [], [], []
            for i in range(3):
                for j in range(3):
                    lo, mid, hi = x[i][j]
                    tops.append(jnp.maximum(jnp.maximum(lo, hi), mid))
                    bottoms.append(jnp.minimum(jnp.minimum(lo, hi), mid))
                    line = (lo + hi) + 4.0 * mid
                    weight = NODE_WEIGHTS[i] * NODE_WEIGHTS[j]
                    averages.append(line if weight == 1.0 else weight * line)
            average = tree(jnp.add, averages) * (1.0 / 216.0)
            largest = tree(jnp.maximum, tops)
            smallest = tree(jnp.minimum, bottoms)
            lowest = bounds[f, r, 2]
            highest = bounds[f, r, 3]
            upper = (jnp.maximum(highest - average, 0.0) + SOFTNESS) / (largest - average + SOFTNESS)
            lower = (jnp.maximum(average - lowest, 0.0) + SOFTNESS) / (average - smallest + SOFTNESS)
            scaling = jnp.minimum(1.0, jnp.minimum(upper, lower))
            offset = average - scaling * average
            for i in range(3):
                for j in range(3):
                    for k in range(3):
                        x[i][j][k] = scaling * x[i][j][k] + offset
                        state[target, f, i, j, k, r] = x[i][j][k]
            pack_faces(n + FIELDS, r, x)
            pack_bounds(n + FIELDS, f, r, scaling * smallest + offset, scaling * largest + offset)

    def stage(n, _):
        t = lax.div(n, FIELDS)
        f = n - FIELDS * t
        part = lax.rem(t, 3)

        @pl.when(t == 0)
        def _():
            begin(f)

        for_faces(n, part, lambda copy: copy.wait_recv())

        @pl.when(part == 0)
        def _():
            gather_bounds(n, f)

        outer_part(n, t, f)

        @pl.when(t < STAGES - 1)
        def _():
            for_faces(n + FIELDS, lax.rem(part + 1, 3), lambda copy: copy.start())
            inner_part(t + 1, f)

        @pl.when(t == STAGES - 1)
        def _():
            pltpu.make_async_copy(state.at[0, f], out_hbm.at[f], store_sem.at[f]).start()

        return 0

    lax.fori_loop(0, STAGES * FIELDS, stage, 0)

    speed_y.wait_send()
    speed_x.wait_send()
    for phase, received in enumerate((near_max, far_max)):
        n = received.shape[0]
        if n > 1:
            pltpu.make_async_copy(
                received.at[pl.ds(1, n - 1)], received.at[pl.ds(1, n - 1)], max_send_sem.at[phase]
            ).wait()

    def drain(n, _):
        for_faces(n, lax.rem(lax.div(n, FIELDS), 3), lambda copy: copy.wait_send())
        return 0

    lax.fori_loop(0, STAGES * FIELDS, drain, 0)
    for f in range(FIELDS):
        pltpu.make_async_copy(state.at[0, f], out_hbm.at[f], store_sem.at[f]).wait()


def solution(mesh):
    n_slab, n_sub = mesh.shape["slab"], mesh.shape["sub"]
    n_near = 16
    n_far = n_slab * n_sub // n_near

    def on_device(fields, speeds):
        vmem = lambda *shape: pltpu.VMEM(shape, jnp.float32)
        dma = lambda *shape: pltpu.SemaphoreType.DMA(shape)
        return pl.pallas_call(
            functools.partial(kernel, n_slab, n_sub),
            out_shape=jax.ShapeDtypeStruct(fields.shape, fields.dtype),
            in_specs=[pl.BlockSpec(memory_space=pltpu.HBM)] * 2,
            out_specs=pl.BlockSpec(memory_space=pl.ANY),
            scratch_shapes=[
                vmem(3, FIELDS, 3, 3, 3, ROWS, 8, 128),
                vmem(FIELDS, 3, 3, 3, ROWS, 8, 128),
                vmem(3, ROWS, 8, 128),
                vmem(FIELDS, ROWS, 4, 8, 128),
                vmem(24 + 2 * ROWS, 8, 128),
                vmem((STAGES + 1) * FIELDS, 2, X_TILES, 8, 128),
                vmem(STAGES * FIELDS, 2, X_TILES, 8, 128),
                vmem((STAGES + 1) * FIELDS, 2, Y_ROWS, 128),
                vmem(STAGES * FIELDS, 2, Y_ROWS, 128),
                vmem(8, 128),
                vmem(8, 128),
                vmem(8, 128),
                vmem(n_near, 1, 128),
                vmem(n_far, 1, 128),
                vmem(2, 1, 128),
                dma(FIELDS + 1),
                dma(FIELDS),
                dma(STAGES * FIELDS, 4),
                dma(STAGES * FIELDS, 4),
                dma(2),
                dma(2),
                dma(2),
                dma(2),
            ],
            compiler_params=pltpu.CompilerParams(
                collective_id=1, has_side_effects=True, vmem_limit_bytes=60 * 1024 * 1024
            ),
            name="remap",
        )(fields, speeds)

    spec = P(None, None, None, None, "slab", "sub", None)
    return jax.shard_map(
        on_device,
        mesh=mesh,
        in_specs=(spec, P(None, "slab", "sub", None)),
        out_specs=spec,
        check_vma=False,
    )
```

time: 89.2 us -> 87.8 us (0.984); the launches traced: 87.8 us -> 87.6 us
  no operation moved by 1% of the time
where the time goes in v3:
time: 87.8 us; the launch traced here: 87.6 us
  Pallas kernels  85.6 us (97%)
  local copies, waits for them, and re-layouts  1.97 us (2%)
    pallas_call x1, Pallas kernels, on_device(): pl.pallas_call(functools.partial(kernel, n_slab, n_sub), out_shape=jax.Sh...  85.6 us
    unnamed x1, local copies, waits for them, and re-layouts  1.97 us

profile of v3, /device:TPU:1, one launch (start us, length us, event | category | flops | bytes accessed | tf_op | source)
XLA Modules:
  0.0 87.6 jit_solution(8606813569268594191)
XLA Ops:
  0.0 85.6 %remap.1 = f32[3,3,3,3,2,8,128]{6,5,4,3,2,1,0:T(8,128)} custom-call(f32[3,3,3,3,2,8,128]{6,5,4,3,2,1,0:T(8,128)} %fields_hbm.1, f32[3,2,8,128]{3,2,1,0:T(8,128)} %speeds_hbm.1), custom_call_target="tpu_custom_call" | custom-call | tf_op jit(solution)/shard_map/remap/pallas_call | solution.py:480
  85.6 2.0 %copy.4 = f32[3,3,3,3,2,8,128]{6,5,4,3,2,1,0:T(8,128)} copy(f32[3,3,3,3,2,8,128]{6,5,4,3,2,1,0:T(8,128)} %remap.1) | data formatting | bytes 1327104

commit v4 on v3

--- a/solution.py
+++ b/solution.py
@@ -51,7 +51,7 @@
     n_sub,
     fields_hbm,
     speeds_hbm,
-    out_hbm,
+    out,
     state,
     partial,
     speeds,
@@ -67,8 +67,8 @@
     near_max,
     far_max,
     max_send,
+    measure,
     load_sem,
-    store_sem,
     face_send_sem,
     face_recv_sem,
     speed_send_sem,
@@ -110,13 +110,10 @@
         neighbours.append((axis, odd, {axis: jnp.where(odd == 1, before, after)}))
     previous = {"sub": {"sub": shifted(sub, n_sub - 1, n_sub)}, "slab": {"slab": shifted(slab, n_slab - 1, n_slab)}}
 
-    load_speeds = pltpu.make_async_copy(speeds_hbm, speeds, load_sem.at[FIELDS])
+    load_speeds = pltpu.make_async_copy(speeds_hbm, speeds, load_sem.at[0])
     load_speeds.start()
-    loads = []
-    for f in range(FIELDS):
-        load = pltpu.make_async_copy(fields_hbm.at[f], state.at[0, f], load_sem.at[f])
-        load.start()
-        loads.append(load)
+    load_fields = pltpu.make_async_copy(fields_hbm, state.at[0], load_sem.at[1])
+    load_fields.start()
 
     barrier = pltpu.get_barrier_semaphore()
     greeted = [device for _, _, device in neighbours] + [device for _, device in far + near]
@@ -148,7 +145,7 @@
 
     def face_copies(n, with_bounds):
         copies = []
-        for slot, (axis, way, device) in enumerate(neighbours):
+        for axis, way, device in neighbours:
             if axis == "sub":
                 sent, received, size = send_y, recv_y, Y_USED if with_bounds else Y_NODES
             else:
@@ -157,24 +154,36 @@
                 pltpu.make_async_remote_copy(
                     src_ref=sent.at[n, way, pl.ds(0, size)],
                     dst_ref=received.at[n, way, pl.ds(0, size)],
-                    send_sem=face_send_sem.at[n, slot],
-                    recv_sem=face_recv_sem.at[n, slot],
+                    send_sem=face_send_sem.at[lax.rem(n, 2 * FIELDS)],
+                    recv_sem=face_recv_sem.at[lax.rem(n, 2 * FIELDS)],
                     device_id=device,
                     device_id_type=MESH,
                 )
             )
         return copies
 
-    def for_faces(n, part, action):
+    def start_faces(n, part):
         @pl.when(part == 0)
         def _():
             for copy in face_copies(n, True):
-                action(copy)
+                copy.start()
 
         @pl.when(part != 0)
         def _():
             for copy in face_copies(n, False):
-                action(copy)
+                copy.start()
+
+    def wait_rows(rows, sem):
+        pltpu.make_async_copy(measure.at[pl.ds(0, rows)], measure.at[pl.ds(0, rows)], sem).wait()
+
+    def wait_faces(n, part, sems):
+        @pl.when(part == 0)
+        def _():
+            wait_rows(2 * (Y_USED + 8 * X_TILES), sems.at[lax.rem(n, 2 * FIELDS)])
+
+        @pl.when(part != 0)
+        def _():
+            wait_rows(2 * (Y_NODES + 8 * X_NODES), sems.at[lax.rem(n, 2 * FIELDS)])
 
     def pack_faces(n, r, values):
         for i in range(3):
@@ -216,8 +225,7 @@
             copy.start()
         return 0
 
-    for load in loads:
-        load.wait()
+    load_fields.wait()
     lax.fori_loop(0, FIELDS, first_faces, 0)
 
     row_at = lax.broadcasted_iota(jnp.int32, (8, 128), 0)
@@ -430,7 +438,7 @@
         def _():
             begin(f)
 
-        for_faces(n, part, lambda copy: copy.wait_recv())
+        wait_faces(n, part, face_recv_sem)
 
         @pl.when(part == 0)
         def _():
@@ -440,16 +448,16 @@
 
         @pl.when(t < STAGES - 1)
         def _():
-            for_faces(n + FIELDS, lax.rem(part + 1, 3), lambda copy: copy.start())
+            start_faces(n + FIELDS, lax.rem(part + 1, 3))
             inner_part(t + 1, f)
 
+        wait_faces(n, part, face_send_sem)
+
         @pl.when(t == STAGES - 1)
         def _():
-            pltpu.make_async_copy(state.at[0, f], out_hbm.at[f], store_sem.at[f]).start()
+            out[f] = state[0, f]
 
         return 0
-
-    lax.fori_loop(0, STAGES * FIELDS, stage, 0)
 
     speed_y.wait_send()
     speed_x.wait_send()
@@ -460,13 +468,7 @@
                 received.at[pl.ds(1, n - 1)], received.at[pl.ds(1, n - 1)], max_send_sem.at[phase]
             ).wait()
 
-    def drain(n, _):
-        for_faces(n, lax.rem(lax.div(n, FIELDS), 3), lambda copy: copy.wait_send())
-        return 0
-
-    lax.fori_loop(0, STAGES * FIELDS, drain, 0)
-    for f in range(FIELDS):
-        pltpu.make_async_copy(state.at[0, f], out_hbm.at[f], store_sem.at[f]).wait()
+    lax.fori_loop(0, STAGES * FIELDS, stage, 0)
 
 
 def solution(mesh):
@@ -479,9 +481,9 @@
         dma = lambda *shape: pltpu.SemaphoreType.DMA(shape)
         return pl.pallas_call(
             functools.partial(kernel, n_slab, n_sub),
-            out_shape=jax.ShapeDtypeStruct(fields.shape, fields.dtype),
+            out_shape=pltpu.VMEM(fields.shape, fields.dtype),
             in_specs=[pl.BlockSpec(memory_space=pltpu.HBM)] * 2,
-            out_specs=pl.BlockSpec(memory_space=pl.ANY),
+            out_specs=pl.BlockSpec(memory_space=pltpu.VMEM),
             scratch_shapes=[
                 vmem(3, FIELDS, 3, 3, 3, ROWS, 8, 128),
                 vmem(FIELDS, 3, 3, 3, ROWS, 8, 128),
@@ -498,10 +500,10 @@
                 vmem(n_near, 1, 128),
                 vmem(n_far, 1, 128),
                 vmem(2, 1, 128),
-                dma(FIELDS + 1),
-                dma(FIELDS),
-                dma(STAGES * FIELDS, 4),
-                dma(STAGES * FIELDS, 4),
+                vmem(2 * (Y_USED + 8 * X_TILES) + 4, 128),
+                dma(2),
+                dma(2 * FIELDS),
+                dma(2 * FIELDS),
                 dma(2),
                 dma(2),
                 dma(2),

time: 87.8 us -> 84.2 us (0.959)
  Pallas kernels: 85.6 us -> 83.1 us
  local copies, waits for them, and re-layouts: 1.97 us -> 0.84 us
    pallas_call x1, Pallas kernels: 85.6 us -> 83.1 us  [on_device(): pl.pallas_call(functools.partial(kernel, n_slab, n_sub), out_shape=pltpu....]
    unnamed x1, local copies, waits for them, and re-layouts: 1.97 us -> 0.84 us
where the time goes in v4:
time: 84.2 us; the launch traced here: 84 us
  Pallas kernels  83.1 us (99%)
    pallas_call x1, Pallas kernels, on_device(): pl.pallas_call(functools.partial(kernel, n_slab, n_sub), out_shape=pltpu....  83.1 us

profile of v4, /device:TPU:1, one launch (start us, length us, event | category | flops | bytes accessed | tf_op | source)
XLA Modules:
  0.0 84.0 jit_solution(15009162205712809907)
XLA Ops:
  0.0 83.1 %remap.1 = f32[3,3,3,3,2,8,128]{6,5,4,3,2,1,0:T(8,128)S(1)} custom-call(f32[3,3,3,3,2,8,128]{6,5,4,3,2,1,0:T(8,128)} %fields_hbm.1, f32[3,2,8,128]{3,2,1,0:T(8,128)} %speeds_hbm.1), custom_call_target="tpu_custom_call" | custom-call | tf_op jit(solution)/shard_map/remap/pallas_call | solution.py:482
  83.1 0.8 %copy.4 = f32[3,3,3,3,2,8,128]{6,5,4,3,2,1,0:T(8,128)} copy(f32[3,3,3,3,2,8,128]{6,5,4,3,2,1,0:T(8,128)S(1)} %remap.1) | data formatting | bytes 1327104

commit v5 on v4

--- a/solution.py
+++ b/solution.py
@@ -17,15 +17,6 @@
 MESH = pl.DeviceIdType.MESH
 X_TILES, X_NODES = 11, 9
 Y_ROWS, Y_USED, Y_NODES = 24, 22, 18
-
-
-def ring_distance(by, size):
-    return min(by, size - by)
-
-
-def farthest_first(outer, inner, hops):
-    steps = [(a, b) for a in range(outer) for b in range(inner) if a or b]
-    return sorted(steps, key=lambda step: -hops(*step))
 
 
 def tree(pick, values):
@@ -86,22 +77,26 @@
 
     z, l = lax.div(slab, 8), lax.rem(slab, 8)
     x, h = lax.div(sub, 2), lax.rem(sub, 2)
-    along_l = [8 * z + shifted(l, by, 8) for by in range(8)]
-    along_h = [2 * x + shifted(h, by, 2) for by in range(2)]
-    along_z = [8 * shifted(z, by, n_z) + l for by in range(n_z)]
-    along_x = [2 * shifted(x, by, n_x) + h for by in range(n_x)]
-    near = [
-        (2 * by_l + by_h, {"slab": along_l[by_l], "sub": along_h[by_h]})
-        for by_h, by_l in farthest_first(
-            2, 8, lambda by_h, by_l: ring_distance((4 * by_h + by_l // 2) % 8, 8)
-        )
-    ]
-    far = [
-        (n_x * by_z + by_x, {"slab": along_z[by_z], "sub": along_x[by_x]})
-        for by_z, by_x in farthest_first(
-            n_z, n_x, lambda by_z, by_x: ring_distance(by_z, n_z) + ring_distance(by_x, n_x)
-        )
-    ]
+    n_near, n_far = near_max.shape[0], far_max.shape[0]
+
+    def near_device(by):
+        at = shifted(8 * h + l, by, n_near)
+        half = jnp.where(at >= 8, 1, 0)
+        return {"slab": 8 * z + at - 8 * half, "sub": 2 * x + half}
+
+    def far_device(by):
+        at = shifted(n_x * z + x, by, n_far)
+        plane = lax.div(at, n_x)
+        return {"slab": 8 * plane + l, "sub": 2 * (at - n_x * plane) + h}
+
+    def for_partners(n, action):
+        def body(step, _):
+            away = lax.div(step + 1, 2)
+            action(n // 2 + jnp.where(lax.rem(step, 2) == 1, -away, away))
+            return 0
+
+        lax.fori_loop(0, n - 1, body, 0)
+
     neighbours = []
     for axis, at, size, odd in (("sub", sub, n_sub, h), ("slab", slab, n_slab, lax.rem(l, 2))):
         after = shifted(at, 1, size)
@@ -110,19 +105,23 @@
         neighbours.append((axis, odd, {axis: jnp.where(odd == 1, before, after)}))
     previous = {"sub": {"sub": shifted(sub, n_sub - 1, n_sub)}, "slab": {"slab": shifted(slab, n_slab - 1, n_slab)}}
 
+
+    barrier = pltpu.get_barrier_semaphore()
+    def greet(device):
+        pl.semaphore_signal(barrier, inc=1, device_id=device, device_id_type=MESH)
+
+    for _, _, device in neighbours:
+        greet(device)
     load_speeds = pltpu.make_async_copy(speeds_hbm, speeds, load_sem.at[0])
     load_speeds.start()
     load_fields = pltpu.make_async_copy(fields_hbm, state.at[0], load_sem.at[1])
     load_fields.start()
-
-    barrier = pltpu.get_barrier_semaphore()
-    greeted = [device for _, _, device in neighbours] + [device for _, device in far + near]
-    for device in greeted:
-        pl.semaphore_signal(barrier, inc=1, device_id=device, device_id_type=MESH)
+    for_partners(n_far, lambda by: greet(far_device(by)))
+    for_partners(n_near, lambda by: greet(near_device(by)))
     load_speeds.wait()
     for r in range(ROWS):
         speed_send[r : r + 1, :] = speeds[1, r, 0:1, :]
-    pl.semaphore_wait(barrier, len(greeted))
+    pl.semaphore_wait(barrier, len(neighbours) + (n_far - 1) + (n_near - 1))
 
     speed_y = pltpu.make_async_remote_copy(
         src_ref=speed_send,
@@ -221,6 +220,9 @@
             pack_bounds(
                 f, f, r, tree(jnp.minimum, flat), tree(jnp.maximum, flat)
             )
+        return 0
+
+    def send_first(f, _):
         for copy in face_copies(f, True):
             copy.start()
         return 0
@@ -326,22 +328,25 @@
                             x = share * state[0, f, i, j, k, r] + rest * x
                         partial[f, i, j, k, r] = x
 
-    for phase, (received, partners) in enumerate(((near_max, near), (far_max, far))):
+    for phase, (received, device_of) in enumerate(((near_max, near_device), (far_max, far_device))):
         n = received.shape[0]
         received[0] = fast
         if n > 1:
             max_send[phase] = fast
-            for slot, device in partners:
-                copy = pltpu.make_async_remote_copy(
+
+            def send(by):
+                pltpu.make_async_remote_copy(
                     src_ref=max_send.at[phase],
-                    dst_ref=received.at[slot],
+                    dst_ref=received.at[by],
                     send_sem=max_send_sem.at[phase],
                     recv_sem=max_recv_sem.at[phase],
-                    device_id=device,
+                    device_id=device_of(by),
                     device_id_type=MESH,
-                )
-                copy.start()
+                ).start()
+
+            for_partners(n, send)
             if phase == 0:
+                lax.fori_loop(0, FIELDS, send_first, 0)
                 for at, v in enumerate(coefficients()):
                     coef[at] = v
                 lax.fori_loop(0, FIELDS, lambda f, _: (inner_part(0, f, True), 0)[1], 0)

time: 84.2 us -> 82.8 us (0.983)
  Pallas kernels: 83.1 us -> 81.8 us
    pallas_call x1, Pallas kernels: 83.1 us -> 81.8 us  [on_device(): pl.pallas_call(functools.partial(kernel, n_slab, n_sub), out_shape=pltpu....]
where the time goes in v5:
time: 82.8 us; the launch traced here: 82.7 us
  Pallas kernels  81.8 us (99%)
  local copies, waits for them, and re-layouts  0.84 us (1%)
    pallas_call x1, Pallas kernels, on_device(): pl.pallas_call(functools.partial(kernel, n_slab, n_sub), out_shape=pltpu....  81.8 us

profile of v5, /device:TPU:1, one launch (start us, length us, event | category | flops | bytes accessed | tf_op | source)
XLA Modules:
  0.0 82.7 jit_solution(1215084670341198488)
XLA Ops:
  0.0 81.8 %remap.1 = f32[3,3,3,3,2,8,128]{6,5,4,3,2,1,0:T(8,128)S(1)} custom-call(f32[3,3,3,3,2,8,128]{6,5,4,3,2,1,0:T(8,128)} %fields_hbm.1, f32[3,2,8,128]{3,2,1,0:T(8,128)} %speeds_hbm.1), custom_call_target="tpu_custom_call" | custom-call | tf_op jit(solution)/shard_map/remap/pallas_call | solution.py:487
  81.8 0.8 %copy.4 = f32[3,3,3,3,2,8,128]{6,5,4,3,2,1,0:T(8,128)} copy(f32[3,3,3,3,2,8,128]{6,5,4,3,2,1,0:T(8,128)S(1)} %remap.1) | data formatting | bytes 1327104

commit v6 on v5

--- a/solution.py
+++ b/solution.py
@@ -142,9 +142,11 @@
     speed_y.start()
     speed_x.start()
 
-    def face_copies(n, with_bounds):
+    def face_copies(n, with_bounds, axes=("sub", "slab")):
         copies = []
         for axis, way, device in neighbours:
+            if axis not in axes:
+                continue
             if axis == "sub":
                 sent, received, size = send_y, recv_y, Y_USED if with_bounds else Y_NODES
             else:
@@ -161,15 +163,15 @@
             )
         return copies
 
-    def start_faces(n, part):
+    def start_faces(n, part, axes):
         @pl.when(part == 0)
         def _():
-            for copy in face_copies(n, True):
+            for copy in face_copies(n, True, axes):
                 copy.start()
 
         @pl.when(part != 0)
         def _():
-            for copy in face_copies(n, False):
+            for copy in face_copies(n, False, axes):
                 copy.start()
 
     def wait_rows(rows, sem):
@@ -184,20 +186,20 @@
         def _():
             wait_rows(2 * (Y_NODES + 8 * X_NODES), sems.at[lax.rem(n, 2 * FIELDS)])
 
-    def pack_faces(n, r, values):
+    def pack_sub(n, r, values):
         for i in range(3):
-            for j in range(3):
-                for k in range(3):
-                    v = values[i][j][k]
-                    if i == 2 and r == ROWS - 1:
-                        send_x[n, 0, 3 * j + k] = v
-                    if i == 0 and r == 0:
-                        send_x[n, 1, 3 * j + k] = v
-                    at = 9 * r + 3 * i + k
-                    if j == 2:
-                        send_y[n, 0, at : at + 1, :] = v[7:8, :]
-                    if j == 0:
-                        send_y[n, 1, at : at + 1, :] = v[0:1, :]
+            for k in range(3):
+                at = 9 * r + 3 * i + k
+                send_y[n, 0, at : at + 1, :] = values[i][2][k][7:8, :]
+                send_y[n, 1, at : at + 1, :] = values[i][0][k][0:1, :]
+
+    def pack_slab(n, r, values):
+        for j in range(3):
+            for k in range(3):
+                if r == ROWS - 1:
+                    send_x[n, 0, 3 * j + k] = values[2][j][k]
+                if r == 0:
+                    send_x[n, 1, 3 * j + k] = values[0][j][k]
 
     def pack_bounds(n, f, r, lowest, highest):
         for which, v in ((0, lowest), (1, highest)):
@@ -216,7 +218,8 @@
                 [[state[0, f, i, j, k, r] for k in range(3)] for j in range(3)] for i in range(3)
             ]
             flat = [values[i][j][k] for i in range(3) for j in range(3) for k in range(3)]
-            pack_faces(f, r, values)
+            pack_sub(f, r, values)
+            pack_slab(f, r, values)
             pack_bounds(
                 f, f, r, tree(jnp.minimum, flat), tree(jnp.maximum, flat)
             )
@@ -391,6 +394,7 @@
     def outer_part(n, t, f):
         target = lax.rem(t + 1, 3)
         _, rest = shares(t)
+        limited = []
         for r in range(ROWS):
             x = [
                 [[partial[f, i, j, k, r] for k in range(3)] for j in range(3)] for i in range(3)
@@ -430,9 +434,20 @@
                 for j in range(3):
                     for k in range(3):
                         x[i][j][k] = scaling * x[i][j][k] + offset
-                        state[target, f, i, j, k, r] = x[i][j][k]
-            pack_faces(n + FIELDS, r, x)
+            pack_sub(n + FIELDS, r, x)
             pack_bounds(n + FIELDS, f, r, scaling * smallest + offset, scaling * largest + offset)
+            limited.append(x)
+
+        @pl.when(t < STAGES - 1)
+        def _():
+            start_faces(n + FIELDS, lax.rem(t + 1, 3), ("sub",))
+
+        for r in range(ROWS):
+            pack_slab(n + FIELDS, r, limited[r])
+            for i in range(3):
+                for j in range(3):
+                    for k in range(3):
+                        state[target, f, i, j, k, r] = limited[r][i][j][k]
 
     def stage(n, _):
         t = lax.div(n, FIELDS)
@@ -453,7 +468,7 @@
 
         @pl.when(t < STAGES - 1)
         def _():
-            start_faces(n + FIELDS, lax.rem(part + 1, 3))
+            start_faces(n + FIELDS, lax.rem(part + 1, 3), ("slab",))
             inner_part(t + 1, f)
 
         wait_faces(n, part, face_send_sem)

time: 82.8 us -> 83.3 us (level)
  no operation moved by 1% of the time
where the time goes in v6:
time: 83.3 us; the launch traced here: 82.5 us
  Pallas kernels  81.6 us (98%)
  local copies, waits for them, and re-layouts  0.84 us (1%)
    pallas_call x1, Pallas kernels, on_device(): pl.pallas_call(functools.partial(kernel, n_slab, n_sub), out_shape=pltpu....  81.6 us

profile of v6, /device:TPU:1, one launch (start us, length us, event | category | flops | bytes accessed | tf_op | source)
XLA Modules:
  0.0 82.5 jit_solution(11755249700835199340)
XLA Ops:
  0.0 81.6 %remap.1 = f32[3,3,3,3,2,8,128]{6,5,4,3,2,1,0:T(8,128)S(1)} custom-call(f32[3,3,3,3,2,8,128]{6,5,4,3,2,1,0:T(8,128)} %fields_hbm.1, f32[3,2,8,128]{3,2,1,0:T(8,128)} %speeds_hbm.1), custom_call_target="tpu_custom_call" | custom-call | tf_op jit(solution)/shard_map/remap/pallas_call | solution.py:502
  81.6 0.8 %copy.4 = f32[3,3,3,3,2,8,128]{6,5,4,3,2,1,0:T(8,128)} copy(f32[3,3,3,3,2,8,128]{6,5,4,3,2,1,0:T(8,128)S(1)} %remap.1) | data formatting | bytes 1327104
